TPU v7x, 32 devices: a whole 2x2x4 slice. The times are simulated.
32 devices in a mesh: gx: 8 (over y, x, core), gy: 4 (over z).
Axes of the slice: x: 2, y: 2, z: 4, core: 2. Of those that a mesh axis runs over, the one named last changes fastest.
Arguments:
- ends: float32 [6, 262144], P(None, ('gx', 'gy')), may hold values from -0.05 to 1.05, as said below
- burgers: float32 [3, 262144], P(None, ('gx', 'gy')), may hold values from -4 to 4
- seg_cell: int32 [262144], P(('gx', 'gy')), may hold values from 0 to 255, as said below
- send_blocks: int32 [32, 4, 24], P(('gx', 'gy')), may hold values from 0 to 63
- send_count: int32 [32, 4], P(('gx', 'gy')), may hold values from 1 to 24, as said below
- pair_list: int32 [32, 64, 2], P(('gx', 'gy')), may hold values from 0 to 159, as said below
- pair_count: int32 [32], replicated, may hold values from 16 to 64, as said below
Outputs:
- end_force: float32 [6, 262144], P(None, ('gx', 'gy'))
Inputs may be any that keep to these rules, and one draw needn't show every extreme that they name: `ends`: each segment's midpoint lies inside the coarse cell seg_cell names and inside its own domain's region. `seg_cell`: the coarse cell holding the segment's midpoint. `send_count`: every domain has a neighbour to which exactly 24 slots are used. `pair_list`: first entry a local block below 64; second an extended block; slots beyond the count are ignored. `pair_count`: some domain has exactly 64.
All inputs are finite; a program needn't handle non-finite values.
Results may differ from a plain program's by a relative error of at most 0.0003.
Values sent between devices are 32-bit elements; how exact they have to be, the bound alone decides.
A program may use at most 64 MiB of HBM per device.

v0:
```python
import jax
import jax.numpy as jnp
from jax import lax
from jax.sharding import PartitionSpec as P

CELL_XY = 8
CELL_Z = 4
CELLS = 256


CORE_SQ = 2.5e-05
NEAR_COEF = 0.2
FAR_COEF = 0.2


def padded(value, sides, width):
    for axis, dim in sides:
        peers, length = (lax.axis_size(axis), value.shape[dim])
        up = [(i, (i + 1) % peers) for i in range(peers - 1)]
        down = [(j, i) for i, j in up]
        last = lax.slice_in_dim(value, length - width, length, axis=dim)
        leading = lax.slice_in_dim(value, 0, width, axis=dim)
        before = lax.ppermute(last, axis, up)
        after = lax.ppermute(leading, axis, down)
        value = jnp.concatenate([before, value, after], axis=dim)
    return value


def pair_forces(block_s, block_t, same):
    mid_s = 0.5 * (block_s[0:3] + block_s[3:6])
    line_s = block_s[3:6] - block_s[0:3]
    burg_s = block_s[6:9]
    mid_t = 0.5 * (block_t[0:3] + block_t[3:6])
    line_t = block_t[3:6] - block_t[0:3]
    burg_t = block_t[6:9]
    rel = mid_t[:, None, :] - mid_s[:, :, None]
    quad = jnp.sum(rel * rel, 0) + CORE_SQ
    inv = lax.rsqrt(quad)
    inv3 = inv * inv * inv
    dot_bb = jnp.sum(burg_s[:, :, None] * burg_t[:, None, :], 0)
    dot_ll = jnp.sum(line_s[:, :, None] * line_t[:, None, :], 0)
    dot_bl = jnp.sum(burg_s[:, :, None] * line_t[:, None, :], 0)
    dot_lb = jnp.sum(line_s[:, :, None] * burg_t[:, None, :], 0)
    lane = jnp.arange(128)
    upper = (lane[:, None] < lane[None, :]).astype(jnp.float32)
    keep = jnp.where(same > 0.5, upper, jnp.ones_like(upper))
    coef = NEAR_COEF * (dot_bb * dot_ll + dot_bl * dot_lb) * inv3 * keep
    push = coef[None] * rel
    len_s = jnp.sum(line_s * line_s, 0)
    len_t = jnp.sum(line_t * line_t, 0)
    share_s = 0.5 * jnp.sum(line_s[:, :, None] * rel, 0) / (quad + len_s[:, None])
    share_t = -0.5 * jnp.sum(line_t[:, None, :] * rel, 0) / (quad + len_t[None, :])
    first_s = -jnp.sum((0.5 - share_s)[None] * push, 2)
    second_s = -jnp.sum((0.5 + share_s)[None] * push, 2)
    first_t = jnp.sum((0.5 - share_t)[None] * push, 1)
    second_t = jnp.sum((0.5 + share_t)[None] * push, 1)
    return (jnp.concatenate([first_s, second_s], 0), jnp.concatenate([first_t, second_t], 0))


def near_loop(extended, pairs, start, stop, totals):

    def step(p, acc):
        left = pairs[p, 0]
        right = pairs[p, 1]
        same = (left == right).astype(jnp.float32)
        force_s, force_t = pair_forces(extended[left], extended[right], same)
        acc = acc.at[left].add(force_s)
        return acc.at[right].add(force_t)

    return lax.fori_loop(start, stop, step, totals)


def moment_terms(ends, burgers):
    line = ends[3:6] - ends[0:3]
    rows = [burgers[p] * line[q] for p in range(3) for q in range(3)]
    rows = rows + [line[q] for q in range(3)]
    return jnp.stack(rows, 0)


def cell_coords(cell):
    return (cell // (CELL_XY * CELL_Z), cell // CELL_Z % CELL_XY, cell % CELL_Z)


def far_field(ends, burgers, seg_cell, moments):
    count = ends.shape[1]
    width = min(512, count)
    groups = count // width
    ends_b = ends.reshape(6, groups, width).transpose(1, 0, 2)
    burg_b = burgers.reshape(3, groups, width).transpose(1, 0, 2)
    cell_b = seg_cell.reshape(groups, width)
    kid = jnp.arange(CELLS, dtype=jnp.int32)
    kx, ky, kz = cell_coords(kid)
    centre = jnp.stack(
        [
            (kx.astype(jnp.float32) + 0.5) / CELL_XY,
            (ky.astype(jnp.float32) + 0.5) / CELL_XY,
            (kz.astype(jnp.float32) + 0.5) / (16 * CELL_Z),
        ],
        0,
    )

    def one(item):
        block_e, block_b, block_c = item
        terms = moment_terms(block_e, block_b)
        weight = jnp.dot(terms.T, moments, precision=lax.Precision.HIGHEST)
        sx, sy, sz = cell_coords(block_c)
        gap = jnp.maximum(
            jnp.maximum(jnp.abs(kx[None, :] - sx[:, None]), jnp.abs(ky[None, :] - sy[:, None])),
            jnp.abs(kz[None, :] - sz[:, None]),
        )
        distant = (gap >= 2).astype(jnp.float32)
        mid = 0.5 * (block_e[0:3] + block_e[3:6])
        rel = centre[:, None, :] - mid[:, :, None]
        quad = jnp.sum(rel * rel, 0) + CORE_SQ
        inv = lax.rsqrt(quad)
        coef = FAR_COEF * weight * inv * inv * inv * distant
        return jnp.sum(coef[None] * rel, 2)

    out = lax.map(one, (ends_b, burg_b, cell_b))
    return out.transpose(1, 0, 2).reshape(3, count)


def cell_moments(ends, burgers, seg_cell):
    local_sum = jax.ops.segment_sum(moment_terms(ends, burgers).T, seg_cell, num_segments=CELLS).T
    return lax.psum(local_sum, ("gx", "gy"))


def on_device(ends, burgers, seg_cell, send_blocks, send_count, pair_list, pair_count):
    seg_here = ends.shape[1]
    blocks = seg_here // 128
    width = send_blocks.shape[2]
    data = jnp.concatenate([ends, burgers], 0).reshape(9, blocks, 128).transpose(1, 0, 2)
    slot_ok = (jnp.arange(width)[None, :] < send_count[0][:, None]).astype(jnp.float32)
    outgoing = data[send_blocks[0]] * slot_ok[:, :, None, None]
    along_x = padded(outgoing[0:2].reshape(2 * width, 9, 128), (("gx", 0),), width)
    along_y = padded(outgoing[2:4].reshape(2 * width, 9, 128), (("gy", 0),), width)
    extended = jnp.concatenate(
        [data, along_x[:width], along_x[3 * width :], along_y[:width], along_y[3 * width :]], 0
    )
    me_index = lax.axis_index("gx") * lax.axis_size("gy") + lax.axis_index("gy")
    mine = pair_count[me_index]
    pairs = pair_list[0]
    totals = jnp.zeros((blocks + 4 * width, 6, 128), jnp.float32)
    totals = near_loop(extended, pairs, 0, mine, totals)
    moments = cell_moments(ends, burgers, seg_cell)
    ghost_force = totals[blocks:].reshape(4, width, 6, 128)
    back_x = padded(jnp.concatenate([ghost_force[0], ghost_force[1]], 0), (("gx", 0),), width)
    back_y = padded(jnp.concatenate([ghost_force[2], ghost_force[3]], 0), (("gy", 0),), width)
    returned = jnp.stack(
        [back_x[:width], back_x[3 * width :], back_y[:width], back_y[3 * width :]], 0
    )
    returned = returned * slot_ok[:, :, None, None]
    local = totals[:blocks].at[send_blocks[0]].add(returned)
    near = local.transpose(1, 0, 2).reshape(6, seg_here)
    far = far_field(ends, burgers, seg_cell, moments)
    return near + jnp.concatenate([0.5 * far, 0.5 * far], 0)


def solution(mesh):
    return jax.shard_map(
        on_device,
        mesh=mesh,
        in_specs=(
            P(None, ("gx", "gy")),
            P(None, ("gx", "gy")),
            P(("gx", "gy")),
            P(("gx", "gy"), None, None),
            P(("gx", "gy"), None),
            P(("gx", "gy"), None, None),
            P(),
        ),
        out_specs=P(None, ("gx", "gy")),
        check_vma=False,
    )
```

profile of v0, /device:TPU:20, one launch (start us, length us, event | category | flops | bytes accessed | tf_op | source)
XLA Modules:
  0.0 740.0 jit_solution(1472638027681553187)
XLA Ops:
  0.0 1.1 pad_maximum_fusion
  2.0 0.7 gather_fusion
  2.9 1.9 collective-permute-start
  4.9 4.5 collective-permute-start.1
  9.4 3.5 collective-permute-start.2
  12.9 2.4 collective-permute-start.3
  16.1 2.6 copy.21
  18.7 44.3 %scatter_custom_fusion.1 = f32[256,12]{1,0:T(8,128)S(1)} fusion(s32[8192]{0:T(1024)S(1)} %copy-done.2, f32[8192,12]{1,0:T(8,128)} %copy.21, f32[]{:T(128)} %constant.272.clone.1), kind=kCustom, calls=%fused_computation.130 | custom fusion | flops 98304 | bytes 12800 | tf_op jit(solution)/shard_map/scatter-add | solution.py:124
  63.1 41.2 %psum.7 = f32[12,256]{0,1:T(8,128)S(1)} all-reduce(f32[12,256]{0,1:T(8,128)S(1)} %bitcast.133), channel_id=1, replica_groups=mesh['gx'=8,'gy'=4] {'gx','gy'}, use_global_device_ids=true, to_apply=%region_19.20 | all-reduce | flops 3072 | bytes 24576 | tf_op jit(solution)/shard_map/psum | solution.py:125
  104.4 41.0 %while.27 = (s32[]{:T(128)}, f32[16,3,512]{2,1,0:T(4,128)}, s32[16,512]{1,0:T(8,128)S(1)}, f32[16,3,512]{2,1,0:T(4,128)S(1)}, f32[16,6,512]{2,1,0:T(8,128)S(1)},...) while((s32[]{:T(128)}, f32[16,3,512]{2,1,0:T(4,128)}, ...), condition=%wide.region_23.24_spmd.clone, body=%wide.region_20.23_spmd.clone.sunk | while | flops 23104772 | bytes 2302141 | solution.py:119
  104.9 1.0 fusion.69
  107.4 1.0 fusion.69
  110.0 1.0 fusion.69
  112.5 1.0 fusion.69
  115.1 1.0 fusion.69
  117.7 1.0 fusion.69
  120.2 1.0 fusion.69
  122.8 1.0 fusion.69
  125.3 1.0 fusion.69
  127.9 1.0 fusion.69
  130.5 1.0 fusion.69
  133.0 1.0 fusion.69
  135.6 1.0 fusion.69
  138.1 1.0 fusion.69
  140.7 1.0 fusion.69
  143.2 1.0 fusion.69
  145.6 0.7 dynamic_slice.39
  146.3 0.9 constant_dynamic-update-slice_fusion.3
  147.2 0.9 constant_dynamic-update-slice_fusion.2
  148.2 0.9 constant_dynamic-update-slice_fusion.1
  149.2 223.8 %while.26 = (s32[]{:T(128)}, f32[160,6,128]{2,1,0:T(8,128)S(1)}, s32[]{:T(128)}, s32[64,2]{0,1:T(2,128)S(1)}, f32[160,9,128]{2,1,0:T(8,128)S(1)}, /*index=5*/s32...) while((s32[]{:T(128)}, f32[160,6,128]{2,1,0:T(8,128)S(1)}, ...), condition=%wide.region_16.17_spmd, body=%wide.region_0.16_spmd.sunk | while | flops 1482034 | bytes 1649015 | solution.py:70
  156.2 0.7 and_reduce_fusion.3
  165.1 0.7 and_reduce_fusion.3
  174.0 0.7 and_reduce_fusion.3
  182.9 0.7 and_reduce_fusion.3
  191.8 0.7 and_reduce_fusion.3
  200.8 0.7 and_reduce_fusion.3
  209.7 0.7 and_reduce_fusion.3
  218.6 0.7 and_reduce_fusion.3
  227.5 0.7 and_reduce_fusion.3
  236.5 0.7 and_reduce_fusion.3
  245.4 0.7 and_reduce_fusion.3
  254.3 0.7 and_reduce_fusion.3
  263.2 0.7 and_reduce_fusion.3
  272.2 0.7 and_reduce_fusion.3
  281.1 0.7 and_reduce_fusion.3
  290.0 0.7 and_reduce_fusion.3
  298.9 0.7 and_reduce_fusion.3
  307.9 0.7 and_reduce_fusion.3
  316.8 0.7 and_reduce_fusion.3
  325.7 0.7 and_reduce_fusion.3
  334.6 0.7 and_reduce_fusion.3
  343.6 0.7 and_reduce_fusion.3
  352.5 0.7 and_reduce_fusion.3
  361.4 0.7 and_reduce_fusion.3
  370.3 0.7 and_reduce_fusion.3
  373.1 127.5 %collective-permute-start.7 = (f32[24,6,128]{2,1,0:T(8,128)S(1)}, f32[24,6,128]{2,1,0:T(8,128)S(1)}, u32[]{:S(2)}, u32[]{:S(2)}) collective-permute-start(f32[24,6,128]{2,1,0:T(8,128)S(1)} %get-tuple-element.356), channel_id=1, source_target_pairs={{1,0},{2,1},{3,2},{5,4},{6,5},{7,6},{9,8},{10,9},{11,10},{13,12},{... | collective-permute-start | bytes 221192 | tf_op jit(solution)/shard_map/ppermute | solution.py:24
  500.6 1.9 collective-permute-start.6
  502.5 225.9 %collective-permute-start.5 = (f32[24,6,128]{2,1,0:T(8,128)S(1)}, f32[24,6,128]{2,1,0:T(8,128)S(1)}, u32[]{:S(2)}, u32[]{:S(2)}) collective-permute-start(f32[24,6,128]{2,1,0:T(8,128)S(1)} %get-tuple-element.358), channel_id=1, source_target_pairs={{4,0},{8,4},{12,8},{16,12},{20,16},{24,20},{28,24},{5,1},{9,5},{13... | collective-permute-start | bytes 221192 | tf_op jit(solution)/shard_map/ppermute | solution.py:24
  728.4 1.9 collective-permute-start.4
  730.3 0.9 broadcast_multiply_fusion.1
  731.3 3.9 collective-permute-done.4
  735.4 3.8 scatter_fusion
  739.2 0.8 maximum_add_fusion
  (457 shorter events, 89.5 us)
Async XLA Ops:
  1.1 0.7 copy-start.5
  1.1 0.8 copy-start.6
  2.7 12.6 %copy-start = (f32[6,8192]{1,0:T(8,128)S(1)}, f32[6,8192]{1,0:T(8,128)}, u32[]{:S(2)}) copy-start(f32[6,8192]{1,0:T(8,128)} %param.15) | copy-start | bytes 589828
  2.8 12.5 %copy-start.2 = (s32[8192]{0:T(1024)S(1)}, s32[8192]{0:T(1024)}, u32[]{:S(2)}) copy-start(s32[8192]{0:T(1024)} %param.17) | copy-start | bytes 98308
  2.9 12.6 %copy-start.1 = (f32[3,8192]{1,0:T(4,128)S(1)}, f32[3,8192]{1,0:T(4,128)}, u32[]{:S(2)}) copy-start(f32[3,8192]{1,0:T(4,128)} %param.16) | copy-start | bytes 294916
  2.9 143.3 %collective-permute-start = (f32[24,9,128]{2,1,0:T(8,128)S(1)}, f32[24,9,128]{2,1,0:T(8,128)}, u32[]{:S(2)}, u32[]{:S(2)}) collective-permute-start(f32[24,9,128]{2,1,0:T(8,128)S(1)} %get-tuple-element.354), channel_id=1, source_target_pairs={{0,4},{4,8},{8,12},{12,16},{16,20},{20,24},{24,28},{1,5},{5,9},{9,... | collective-permute-start | bytes 331784 | tf_op jit(solution)/shard_map/ppermute | solution.py:23
  4.9 142.3 %collective-permute-start.1 = (f32[24,9,128]{2,1,0:T(8,128)S(1)}, f32[24,9,128]{2,1,0:T(8,128)}, u32[]{:S(2)}, u32[]{:S(2)}) collective-permute-start(f32[24,9,128]{2,1,0:T(8,128)S(1)} %get-tuple-element.353), channel_id=1, source_target_pairs={{4,0},{8,4},{12,8},{16,12},{20,16},{24,20},{28,24},{5,1},{9,5},{13... | collective-permute-start | bytes 331784 | tf_op jit(solution)/shard_map/ppermute | solution.py:24
  9.4 138.7 %collective-permute-start.2 = (f32[24,9,128]{2,1,0:T(8,128)S(1)}, f32[24,9,128]{2,1,0:T(8,128)}, u32[]{:S(2)}, u32[]{:S(2)}) collective-permute-start(f32[24,9,128]{2,1,0:T(8,128)S(1)} %get-tuple-element.352), channel_id=1, source_target_pairs={{0,1},{1,2},{2,3},{4,5},{5,6},{6,7},{8,9},{9,10},{10,11},{12,13},{... | collective-permute-start | bytes 331784 | tf_op jit(solution)/shard_map/ppermute | solution.py:23
  12.9 136.2 %collective-permute-start.3 = (f32[24,9,128]{2,1,0:T(8,128)S(1)}, f32[24,9,128]{2,1,0:T(8,128)S(1)}, u32[]{:S(2)}, u32[]{:S(2)}) collective-permute-start(f32[24,9,128]{2,1,0:T(8,128)S(1)} %get-tuple-element.351), channel_id=1, source_target_pairs={{1,0},{2,1},{3,2},{5,4},{6,5},{7,6},{9,8},{10,9},{11,10},{13,12},{... | collective-permute-start | bytes 331784 | tf_op jit(solution)/shard_map/ppermute | solution.py:24
  104.4 41.2 %copy-start.7 = (s32[32]{0:T(128)S(1)}, s32[32]{0:T(128)}, u32[]{:S(2)}) copy-start(s32[32]{0:T(128)} %param.21) | copy-start | bytes 388
  145.5 3.7 copy-start.3
  145.6 3.7 copy-start.4
  373.1 358.2 %collective-permute-start.7 = (f32[24,6,128]{2,1,0:T(8,128)S(1)}, f32[24,6,128]{2,1,0:T(8,128)S(1)}, u32[]{:S(2)}, u32[]{:S(2)}) collective-permute-start(f32[24,6,128]{2,1,0:T(8,128)S(1)} %get-tuple-element.356), channel_id=1, source_target_pairs={{1,0},{2,1},{3,2},{5,4},{6,5},{7,6},{9,8},{10,9},{11,10},{13,12},{... | collective-permute-start | bytes 221192 | tf_op jit(solution)/shard_map/ppermute | solution.py:24
  500.6 230.7 %collective-permute-start.6 = (f32[24,6,128]{2,1,0:T(8,128)S(1)}, f32[24,6,128]{2,1,0:T(8,128)S(1)}, u32[]{:S(2)}, u32[]{:S(2)}) collective-permute-start(f32[24,6,128]{2,1,0:T(8,128)S(1)} %get-tuple-element.357), channel_id=1, source_target_pairs={{0,1},{1,2},{2,3},{4,5},{5,6},{6,7},{8,9},{9,10},{10,11},{12,13},{... | collective-permute-start | bytes 221192 | tf_op jit(solution)/shard_map/ppermute | solution.py:23
  502.5 228.8 %collective-permute-start.5 = (f32[24,6,128]{2,1,0:T(8,128)S(1)}, f32[24,6,128]{2,1,0:T(8,128)S(1)}, u32[]{:S(2)}, u32[]{:S(2)}) collective-permute-start(f32[24,6,128]{2,1,0:T(8,128)S(1)} %get-tuple-element.358), channel_id=1, source_target_pairs={{4,0},{8,4},{12,8},{16,12},{20,16},{24,20},{28,24},{5,1},{9,5},{13... | collective-permute-start | bytes 221192 | tf_op jit(solution)/shard_map/ppermute | solution.py:24
  728.4 6.8 collective-permute-start.4
where the time goes:
time: 747 us; the launch traced here: 740 us
  starting transfers between devices  370 us (50%)
  loops' own time  143 us (19%)
  other arithmetic  131 us (18%)
  blocking collectives  41.2 us (6%)
  local copies, waits for them, and re-layouts  34.9 us (5%)
  matrix products  15.9 us (2%)
    ppermute x4, starting transfers between devices, padded(): after = lax.ppermute(leading, axis, down)  360 us
    another operation x1, loops' own time, near_loop(): return lax.fori_loop(start, stop, step, totals)  142 us
    scatter-add x1, other arithmetic, cell_moments(): jax.ops.segment_sum(moment_terms(ends, burgers).T, seg_cell, num_segments...  44.3 us
    psum x1, blocking collectives, cell_moments(): return lax.psum(local_sum, ('gx', 'gy'))  41.2 us
    another operation x25, other arithmetic  18.5 us
    dot_general x16, matrix products, one(): weight = jnp.dot(terms.T, moments, precision=lax.Precision.HIGHEST)  15.9 us
    scatter-add x25, other arithmetic, step(): acc = acc.at[left].add(force_s)  15.6 us
    dynamic_slice x25, local copies, waits for them, and re-layouts, step(): right = pairs[p, 1]  15.4 us
  transfers between devices with their start and end apart: 8, of which 1 were waited for; matrix products, arithmetic and copies ran while one was open for 13% of the time, Pallas kernels for 0%

commit v1 on v0

v1 whole, which is shorter than its diff:
```python
import functools

import jax
import jax.numpy as jnp
from jax import lax
from jax.experimental import pallas as pl
from jax.experimental.pallas import tpu as pltpu
from jax.sharding import PartitionSpec as P

CELL_XY = 8
CELL_Z = 4
CELLS = 256
LANES = 128
TERM_ROWS = 16
CHUNK = 1024

CORE_SQ = 2.5e-05
NEAR_COEF = 0.2
FAR_COEF = 0.2
F32 = jnp.float32
BF16 = jnp.bfloat16
MESH = pl.DeviceIdType.MESH
VMEM_SPEC = pl.BlockSpec(memory_space=pltpu.VMEM)
SMEM_SPEC = pl.BlockSpec(memory_space=pltpu.SMEM)
VMEM_LIMIT = 48 * 1024 * 1024


def split(value):
    high = value.astype(BF16)
    return high, (value - high.astype(F32)).astype(BF16)


def matmul(a, b):
    return jnp.dot(a, b, preferred_element_type=F32)


def at_block(index, rows=8):
    return pl.ds(pl.multiple_of(index * rows, rows), rows)


def at_lanes(index, lanes=LANES):
    return pl.ds(pl.multiple_of(index * lanes, lanes), lanes)


def prepare(width, slots, counts, ends, burgers, cell, main, bz, terms, outgoing, moments):
    blocks = main.shape[0] // 8

    def rows(b, _):
        at = at_lanes(b)
        first, second, burg = ends[0:3, at], ends[3:6, at], burgers[:, at]
        line = second - first
        base = pl.multiple_of(b * 8, 8)
        main[pl.ds(base, 3), :] = 0.5 * (first + second)
        main[pl.ds(base + 3, 3), :] = line
        main[pl.ds(base + 6, 2), :] = burg[0:2]
        bz[pl.ds(b, 1), :] = burg[2:3]
        for p in range(3):
            terms[3 * p : 3 * p + 3, at] = burg[p : p + 1] * line
        terms[9:12, at] = line
        terms[12:16, at] = jnp.zeros((4, LANES), F32)
        return 0

    lax.fori_loop(0, blocks, rows, 0, unroll=4)

    for r in range(4):

        def gather(g, _):
            block = slots[r * width + g]
            keep = jnp.where(g < counts[r], 1.0, 0.0).astype(F32)
            outgoing[r, at_block(g), :] = main[at_block(block), :] * keep
            outgoing[r, pl.ds(8 * width + g, 1), :] = bz[pl.ds(block, 1), :] * keep
            return 0

        lax.fori_loop(0, width, gather, 0, unroll=4)

    per = CHUNK // LANES
    ids = lax.broadcasted_iota(jnp.int32, (CELLS, LANES), 0)

    def add(c, total):
        at = at_lanes(c, CHUNK)
        high, low = split(terms[:, at])
        both = jnp.concatenate([high, low], 0)
        hot = jnp.concatenate(
            [jnp.where(cell[pl.ds(c * per + k, 1), :] == ids, 1.0, 0.0).astype(BF16) for k in range(per)], 1
        )
        return total + lax.dot_general(both, hot, (((1,), (1,)), ((), ())), preferred_element_type=F32)

    total = lax.fori_loop(0, blocks // per, add, jnp.zeros((2 * TERM_ROWS, CELLS), F32))
    moments[...] = total[:TERM_ROWS] + total[TERM_ROWS:]


def hello(sizes):
    barrier = pltpu.get_barrier_semaphore()
    for axis, size in sizes:
        me = lax.axis_index(axis)
        for step in range(1, size):
            pl.semaphore_signal(
                barrier, inc=1, device_id={axis: lax.rem(me + step, size)}, device_id_type=MESH
            )
    pl.semaphore_wait(barrier, sum(size - 1 for _, size in sizes))


def hello_near(sizes):
    barrier = pltpu.get_barrier_semaphore()
    peers = 0
    for axis, size in sizes:
        me = lax.axis_index(axis)
        peers = peers + jnp.where(me > 0, 1, 0) + jnp.where(me < size - 1, 1, 0)
        for step in (-1, 1):
            there = me > 0 if step < 0 else me < size - 1

            @pl.when(there)
            def _():
                pl.semaphore_signal(barrier, inc=1, device_id={axis: me + step}, device_id_type=MESH)

    pl.semaphore_wait(barrier, peers)


def neighbours(sizes, source, target, send_sem, recv_sem):
    out = []
    for r in range(4):
        axis, size = sizes[r // 2]
        me = lax.axis_index(axis)
        step = 1 if r % 2 else -1
        there = me < size - 1 if r % 2 else me > 0
        peer = jnp.clip(me + step, 0, size - 1)
        copy = pltpu.make_async_remote_copy(
            src_ref=source.at[r],
            dst_ref=target.at[r ^ 1],
            send_sem=send_sem.at[r],
            recv_sem=recv_sem.at[r ^ 1],
            device_id={axis: peer},
            device_id_type=MESH,
        )
        back = pltpu.make_async_remote_copy(
            src_ref=source.at[r],
            dst_ref=target.at[r],
            send_sem=send_sem.at[r],
            recv_sem=recv_sem.at[r],
            device_id={axis: peer},
            device_id_type=MESH,
        )
        out.append((there, copy, back))
    return out


def start_all(copies, target):
    for r, (there, copy, _) in enumerate(copies):

        @pl.when(there)
        def _():
            copy.start()

        @pl.when(jnp.logical_not(there))
        def _():
            target[r] = jnp.zeros(target.shape[1:], F32)


def wait_all(copies):
    for there, copy, back in copies:

        @pl.when(there)
        def _():
            copy.wait_send()
            back.wait_recv()


def exchange(sizes, outgoing, local, ghosts, moments, held_x, held_y, partial, send_sem, recv_sem, sx, rx, sy, ry):
    hello(sizes)
    (ax, nx), (ay, ny) = sizes

    def spread(source, axis, size, held, send, recv):
        me = lax.axis_index(axis)
        copies = []
        for step in range(1, size):
            copy = pltpu.make_async_remote_copy(
                src_ref=source,
                dst_ref=held.at[step - 1],
                send_sem=send.at[step - 1],
                recv_sem=recv.at[step - 1],
                device_id={axis: lax.rem(me + step, size)},
                device_id_type=MESH,
            )
            copy.start()
            copies.append(copy)
        return copies

    first = spread(local, ay, ny, held_y, sy, ry)
    copies = neighbours(sizes, outgoing, ghosts, send_sem, recv_sem)
    start_all(copies, ghosts)
    total = local[...]
    for k, copy in enumerate(first):
        copy.wait()
        total = total + held_y[k]
    partial[...] = total
    second = spread(partial, ax, nx, held_x, sx, rx)
    for k, copy in enumerate(second):
        copy.wait()
        total = total + held_x[k]
    moments[...] = total
    wait_all(copies)


def give_back(sizes, forces, returned, send_sem, recv_sem):
    hello_near(sizes)
    copies = neighbours(sizes, forces, returned, send_sem, recv_sem)
    start_all(copies, returned)
    wait_all(copies)


def interact(width, pairs, count, main, bz, ghosts, cell, terms, moments, own_acc, ghost_acc, ext, sym, acc):
    blocks = main.shape[0] // 8
    total = blocks + 4 * width
    acc[...] = jnp.zeros_like(acc)
    ext[0 : 8 * blocks] = main[...]
    for r in range(4):
        lo = 8 * (blocks + r * width)
        ext[lo : lo + 8 * width] = ghosts[r, 0 : 8 * width]

    def products(tile, base, burg_z):
        lx, ly, lz, bx, by = (tile[k : k + 1] for k in (3, 4, 5, 6, 7))
        sym[pl.ds(base, 1), :] = 2.0 * bx * lx
        sym[pl.ds(base + 1, 1), :] = 2.0 * by * ly
        sym[pl.ds(base + 2, 1), :] = 2.0 * burg_z * lz
        sym[pl.ds(base + 3, 1), :] = bx * ly + by * lx
        sym[pl.ds(base + 4, 1), :] = bx * lz + burg_z * lx
        sym[pl.ds(base + 5, 1), :] = by * lz + burg_z * ly
        sym[pl.ds(base + 6, 1), :] = lx * lx + ly * ly + lz * lz
        sym[pl.ds(base + 7, 1), :] = jnp.zeros((1, LANES), F32)

    def own_products(b, _):
        products(main[at_block(b), :], pl.multiple_of(b * 8, 8), bz[pl.ds(b, 1), :])
        return 0

    lax.fori_loop(0, blocks, own_products, 0, unroll=4)
    for r in range(4):

        def ghost_products(g, _):
            base = pl.multiple_of((blocks + r * width + g) * 8, 8)
            products(ghosts[r, at_block(g), :], base, ghosts[r, pl.ds(8 * width + g, 1), :])
            return 0

        lax.fori_loop(0, width, ghost_products, 0, unroll=4)

    sub = lax.broadcasted_iota(jnp.int32, (8, LANES), 0)
    lane = lax.broadcasted_iota(jnp.int32, (8, LANES), 1)
    ahead = lane - sub
    scale = jnp.where(sub < 3, 0.5 * NEAR_COEF, jnp.where(sub < 6, NEAR_COEF, 0.0)).astype(F32)
    empty = jnp.zeros((8, LANES), F32)

    def pair(p, _):
        left = pairs[2 * p]
        right = pairs[2 * p + 1]
        floor = jnp.where(left == right, 0, -1024)
        source = jnp.concatenate([ext[at_block(left), :], sym[at_block(left), :]], 0)
        cols = source.T
        tile_t = ext[at_block(right), :]
        sym_t = sym[at_block(right), :]
        a_high, a_low = split(cols)
        b_high, b_low = split(jnp.concatenate([empty, sym_t * scale], 0))
        dots = matmul(a_high, b_high) + (matmul(a_high, b_low) + matmul(a_low, b_high))
        mt = [jnp.broadcast_to(tile_t[k : k + 1], (8, LANES)) for k in range(3)]
        lt = [jnp.broadcast_to(tile_t[k + 3 : k + 4], (8, LANES)) for k in range(3)]
        len_t = jnp.broadcast_to(sym_t[6:7], (8, LANES))
        sums_t = [empty] * 6
        columns = []
        for c in range(LANES // 8):
            col = cols[8 * c : 8 * c + 8]
            ms = [col[:, k : k + 1] for k in range(3)]
            ls = [col[:, k + 3 : k + 4] for k in range(3)]
            len_s = col[:, 14:15]
            rel = [mt[k] - ms[k] for k in range(3)]
            quad = rel[0] * rel[0] + rel[1] * rel[1] + rel[2] * rel[2] + CORE_SQ
            inv = lax.rsqrt(quad)
            coef = dots[8 * c : 8 * c + 8] * (inv * inv * inv)
            coef = jnp.where(ahead > floor + 8 * c, coef, 0.0)
            push = [coef * rel[k] for k in range(3)]
            along_s = ls[0] * rel[0] + ls[1] * rel[1] + ls[2] * rel[2]
            along_t = lt[0] * rel[0] + lt[1] * rel[1] + lt[2] * rel[2]
            den_s = quad + len_s
            den_t = quad + len_t
            both = den_s * den_t
            near = pl.reciprocal(both, approx=True)
            near = near * (2.0 - both * near)
            half = 0.5 * near
            share_s = along_s * den_t * half
            share_t = along_t * den_s * half
            skew_s = [share_s * push[k] for k in range(3)]
            for k in range(3):
                sums_t[k] = sums_t[k] + push[k]
                sums_t[k + 3] = sums_t[k + 3] - share_t * push[k]
            made = empty
            for k, value in enumerate(push + skew_s):
                made = jnp.where(lane == k, jnp.sum(value, 1, keepdims=True), made)
            columns.append(made)
        rows_s = jnp.concatenate(columns, 0).T[0:8]
        acc[at_block(left), :] = acc[at_block(left), :] - rows_s
        rows_t = empty
        for k in range(6):
            rows_t = jnp.where(sub == k, jnp.sum(sums_t[k], 0, keepdims=True), rows_t)
        acc[at_block(right), :] = acc[at_block(right), :] + rows_t
        return 0

    lax.fori_loop(0, count[0], pair, 0)

    per_x = CELL_XY * CELL_Z
    groups = per_x // 8
    kz = sub % CELL_Z
    kys = [sub // CELL_Z + (8 // CELL_Z) * j for j in range(groups)]
    z_centre = (kz.astype(F32) + 0.5) / (16 * CELL_Z)
    y_centres = [(ky.astype(F32) + 0.5) / CELL_XY for ky in kys]
    m_high, m_low = split(moments[...].T)

    def far(b, _):
        t_high, t_low = split(terms[:, at_lanes(b)])
        weight = matmul(m_high, t_high) + (matmul(m_high, t_low) + matmul(m_low, t_high))
        tile = main[at_block(b), :]
        mx, my, mz = (jnp.broadcast_to(tile[k : k + 1], (8, LANES)) for k in range(3))
        here = jnp.broadcast_to(cell[pl.ds(b, 1), :], (8, LANES))
        cx, cy, cz = here // per_x, here // CELL_Z % CELL_XY, here % CELL_Z
        rz = z_centre - mz
        rys = [centre - my for centre in y_centres]
        flat = [ry * ry + rz * rz + CORE_SQ for ry in rys]
        gap_z = jnp.abs(kz - cz)
        gaps = [jnp.maximum(jnp.abs(ky - cy), gap_z) for ky in kys]
        sums = [empty] * groups
        fx = empty
        for kx in range(CELL_XY):
            rx = (kx + 0.5) / CELL_XY - mx
            square = rx * rx
            gap_x = jnp.abs(cx - kx)
            plane = empty
            for j in range(groups):
                inv = lax.rsqrt(square + flat[j])
                lo = kx * per_x + 8 * j
                coef = weight[lo : lo + 8] * (inv * inv * inv)
                coef = jnp.where(jnp.maximum(gap_x, gaps[j]) >= 2, coef, 0.0)
                sums[j] = sums[j] + coef
                plane = plane + coef
            fx = fx + rx * plane
        fy, fall = empty, empty
        for j in range(groups):
            fy = fy + rys[j] * sums[j]
            fall = fall + sums[j]
        rows = empty
        for k, value in enumerate((fx, fy, rz * fall)):
            rows = jnp.where(sub == k, jnp.sum(value, 0, keepdims=True), rows)
        own_acc[at_block(b), :] = acc[at_block(b), :] + FAR_COEF * rows
        return 0

    lax.fori_loop(0, blocks, far, 0)
    for r in range(4):
        lo = 8 * (blocks + r * width)
        ghost_acc[r] = acc[lo : lo + 8 * width]


def finish(width, slots, counts, own_acc, returned, out, acc):
    blocks = own_acc.shape[0] // 8
    acc[...] = own_acc[...]
    for r in range(4):

        def add(g, _):
            at = at_block(slots[r * width + g])
            acc[at, :] = acc[at, :] + returned[r, at_block(g), :]
            return 0

        lax.fori_loop(0, counts[r], add, 0)

    def write(b, _):
        tile = acc[at_block(b), :]
        both = 0.5 * tile[0:3]
        out[0:3, at_lanes(b)] = both - tile[3:6]
        out[3:6, at_lanes(b)] = both + tile[3:6]
        return 0

    lax.fori_loop(0, blocks, write, 0, unroll=4)


def shape(*dims):
    return jax.ShapeDtypeStruct(dims, F32)


def on_device(sizes, ends, burgers, seg_cell, send_blocks, send_count, pair_list, pair_count):
    seg_here = ends.shape[1]
    blocks = seg_here // LANES
    width = send_blocks.shape[2]
    sent_rows = 9 * width
    (ax, nx), (ay, ny) = sizes
    slots = send_blocks.reshape(-1)
    counts = send_count.reshape(-1)
    cell = seg_cell.reshape(blocks, LANES)
    here = lax.axis_index(ax) * ny + lax.axis_index(ay)
    count = lax.dynamic_slice(pair_count, (here,), (1,))
    params = pltpu.CompilerParams(vmem_limit_bytes=VMEM_LIMIT)

    main, bz, terms, outgoing, local = pl.pallas_call(
        functools.partial(prepare, width),
        out_shape=(
            shape(blocks * 8, LANES),
            shape(blocks, LANES),
            shape(TERM_ROWS, seg_here),
            shape(4, sent_rows, LANES),
            shape(TERM_ROWS, CELLS),
        ),
        in_specs=[SMEM_SPEC] * 2 + [VMEM_SPEC] * 3,
        out_specs=(VMEM_SPEC,) * 5,
        compiler_params=params,
        name="prepare",
    )(slots, counts, ends, burgers, cell)

    dma = pltpu.SemaphoreType.DMA
    ghosts, moments = pl.pallas_call(
        functools.partial(exchange, sizes),
        out_shape=(shape(4, sent_rows, LANES), shape(TERM_ROWS, CELLS)),
        in_specs=[VMEM_SPEC] * 2,
        out_specs=(VMEM_SPEC,) * 2,
        scratch_shapes=[
            pltpu.VMEM((nx - 1, TERM_ROWS, CELLS), F32),
            pltpu.VMEM((ny - 1, TERM_ROWS, CELLS), F32),
            pltpu.VMEM((TERM_ROWS, CELLS), F32),
            dma((4,)),
            dma((4,)),
            dma((nx - 1,)),
            dma((nx - 1,)),
            dma((ny - 1,)),
            dma((ny - 1,)),
        ],
        compiler_params=pltpu.CompilerParams(
            collective_id=0, has_side_effects=True, vmem_limit_bytes=VMEM_LIMIT
        ),
        name="exchange",
    )(outgoing, local)

    own_acc, ghost_acc = pl.pallas_call(
        functools.partial(interact, width),
        out_shape=(shape(blocks * 8, LANES), shape(4, 8 * width, LANES)),
        in_specs=[SMEM_SPEC] * 2 + [VMEM_SPEC] * 6,
        out_specs=(VMEM_SPEC,) * 2,
        scratch_shapes=[pltpu.VMEM(((blocks + 4 * width) * 8, LANES), F32)] * 3,
        compiler_params=params,
        name="interact",
    )(pair_list.reshape(-1), count, main, bz, ghosts, cell, terms, moments)

    returned = pl.pallas_call(
        functools.partial(give_back, sizes),
        out_shape=shape(4, 8 * width, LANES),
        in_specs=[VMEM_SPEC],
        out_specs=VMEM_SPEC,
        scratch_shapes=[dma((4,)), dma((4,))],
        compiler_params=pltpu.CompilerParams(
            collective_id=1, has_side_effects=True, vmem_limit_bytes=VMEM_LIMIT
        ),
        name="give_back",
    )(ghost_acc)

    return pl.pallas_call(
        functools.partial(finish, width),
        out_shape=shape(6, seg_here),
        in_specs=[SMEM_SPEC] * 2 + [VMEM_SPEC] * 2,
        out_specs=VMEM_SPEC,
        scratch_shapes=[pltpu.VMEM((blocks * 8, LANES), F32)],
        compiler_params=params,
        name="finish",
    )(slots, counts, own_acc, returned)


def solution(mesh):
    sizes = (("gx", mesh.shape["gx"]), ("gy", mesh.shape["gy"]))
    return jax.shard_map(
        functools.partial(on_device, sizes),
        mesh=mesh,
        in_specs=(
            P(None, ("gx", "gy")),
            P(None, ("gx", "gy")),
            P(("gx", "gy")),
            P(("gx", "gy"), None, None),
            P(("gx", "gy"), None),
            P(("gx", "gy"), None, None),
            P(),
        ),
        out_specs=P(None, ("gx", "gy")),
        check_vma=False,
    )
```

time: 747 us -> 132 us (0.18)
  the two profiles are of different devices: /device:TPU:20 before, /device:TPU:0 now
where the time goes in v1:
time: 132 us; the launch traced here: 131 us
  Pallas kernels  126 us (95%)
  local copies, waits for them, and re-layouts  5.21 us (4%)
    pallas_call x1, Pallas kernels, on_device(): pl.pallas_call(functools.partial(give_back, sizes), out_shape=shape(4, 8...  57.5 us
    pallas_call x1, Pallas kernels, on_device(): pl.pallas_call(functools.partial(interact, width), out_shape=(shape(block...  50.6 us
    pallas_call x1, Pallas kernels, on_device(): pl.pallas_call(functools.partial(exchange, sizes), out_shape=(shape(4, se...  12.4 us
    unnamed x15, local copies, waits for them, and re-layouts  4.41 us
    pallas_call x1, Pallas kernels, on_device(): pl.pallas_call(functools.partial(prepare, width), out_shape=(shape(blocks...  3.35 us

profile of v1, /device:TPU:0, one launch (start us, length us, event | category | flops | bytes accessed | tf_op | source)
XLA Modules:
  0.0 131.0 jit_solution(9857291422272482116)
XLA Ops:
  0.0 0.0 copy-start.6
  0.0 0.7 copy-done.6
  0.7 0.6 dynamic_slice.3.count
  1.2 0.0 copy-start.4
  1.2 0.7 copy-done.4
  1.9 0.0 copy-start.5
  1.9 0.1 reshape.12.slots
  2.0 0.6 copy-done.5
  2.6 0.0 copy-start.2
  2.6 0.1 copy.9
  2.7 0.0 copy-start.3
  2.7 0.1 reshape.14.pairs
  2.8 0.5 copy-done.2
  3.4 0.0 copy-done.3
  3.4 0.0 copy-start
  3.4 0.9 copy-done
  4.3 0.0 copy-start.1
  4.3 0.9 copy-done.1
  5.2 3.4 %prepare.1 = (f32[512,128]{1,0:T(8,128)S(1)}, f32[64,128]{1,0:T(8,128)S(1)}, f32[16,8192]{1,0:T(8,128)S(1)}, f32[4,216,128]{2,1,0:T(8,128)S(1)}, f32[16,256]{1,0:T(8,128)S(1)}) custom-call(s32[96]{0:T(128)S(1)} %reshape.12.slots, s32[4]{0:T(128)S(1)} %bitcast.4, f32[6,8192]{1,0:T(8,128)S(1)} %copy-done, f32[3,8192]{1,0:T(4,128)S(1)} %copy-done.1, ...), custom_call_target="tpu_custom_call" | custom-call | tf_op jit(solution)/shard_map/prepare/pallas_call | solution.py:396
  8.6 12.4 %exchange.1 = (f32[4,216,128]{2,1,0:T(8,128)S(1)}, f32[16,256]{1,0:T(8,128)S(1)}) custom-call(f32[4,216,128]{2,1,0:T(8,128)S(1)} %get-tuple-element.16.outgoing, f32[16,256]{1,0:T(8,128)S(1)} %get-tuple-element.17.local), custom_call_target="tpu_custom_call" | custom-call | tf_op jit(solution)/shard_map/exchange/pallas_call | solution.py:412
  20.9 50.6 %interact.1 = (f32[512,128]{1,0:T(8,128)S(1)}, f32[4,192,128]{2,1,0:T(8,128)S(1)}) custom-call(s32[128]{0:T(128)S(1)} %reshape.14.pairs, s32[1]{0:T(128)} %dynamic_slice.3.count, f32[512,128]{1,0:T(8,128)S(1)} %get-tuple-element.14.main, f32[64,128]{1,0:T(8,128)S(1)} %get-tuple-element.15.bz, f32[4,216,128]{2,1,0:T(8,128)S(1)} %get-tuple-element.18.ghosts, ...), custom_call_target="tpu_custom_call" | custom-call | tf_op jit(solution)/shard_map/interact/pallas_call | solution.py:434
  71.6 57.5 %give_back.1.returned = f32[4,192,128]{2,1,0:T(8,128)S(1)} custom-call(f32[4,192,128]{2,1,0:T(8,128)S(1)} %get-tuple-element.22.forces), custom_call_target="tpu_custom_call" | custom-call | tf_op jit(solution)/shard_map/give_back/pallas_call | solution.py:444
  129.1 1.9 %finish.1 = f32[6,8192]{1,0:T(8,128)} custom-call(s32[96]{0:T(128)S(1)} %reshape.12.slots, s32[4]{0:T(128)S(1)} %bitcast.5, f32[512,128]{1,0:T(8,128)S(1)} %get-tuple-element.21.own_acc, f32[4,192,128]{2,1,0:T(8,128)S(1)} %give_back.1.returned), custom_call_target="tpu_custom_call" | custom-call | tf_op jit(solution)/shard_map/finish/pallas_call | solution.py:456
Async XLA Ops:
  0.0 0.7 copy-start.6
  1.2 0.7 copy-start.4
  1.9 0.7 copy-start.5
  2.6 0.8 copy-start.2
  2.7 0.7 copy-start.3
  3.4 1.0 copy-start
  4.3 0.9 copy-start.1

commit v2 on v1

--- a/solution.py
+++ b/solution.py
@@ -208,7 +208,9 @@
     wait_all(copies)
 
 
-def interact(width, pairs, count, main, bz, ghosts, cell, terms, moments, own_acc, ghost_acc, ext, sym, acc):
+def interact(
+    width, pairs, count, main, bz, ghosts, cell, terms, moments, own_acc, ghost_acc, ext, sym, acc, cols, dots, made
+):
     blocks = main.shape[0] // 8
     total = blocks + 4 * width
     acc[...] = jnp.zeros_like(acc)
@@ -217,91 +219,111 @@
         lo = 8 * (blocks + r * width)
         ext[lo : lo + 8 * width] = ghosts[r, 0 : 8 * width]
 
-    def products(tile, base, burg_z):
-        lx, ly, lz, bx, by = (tile[k : k + 1] for k in (3, 4, 5, 6, 7))
-        sym[pl.ds(base, 1), :] = 2.0 * bx * lx
-        sym[pl.ds(base + 1, 1), :] = 2.0 * by * ly
-        sym[pl.ds(base + 2, 1), :] = 2.0 * burg_z * lz
-        sym[pl.ds(base + 3, 1), :] = bx * ly + by * lx
-        sym[pl.ds(base + 4, 1), :] = bx * lz + burg_z * lx
-        sym[pl.ds(base + 5, 1), :] = by * lz + burg_z * ly
-        sym[pl.ds(base + 6, 1), :] = lx * lx + ly * ly + lz * lz
-        sym[pl.ds(base + 7, 1), :] = jnp.zeros((1, LANES), F32)
-
-    def own_products(b, _):
-        products(main[at_block(b), :], pl.multiple_of(b * 8, 8), bz[pl.ds(b, 1), :])
-        return 0
-
-    lax.fori_loop(0, blocks, own_products, 0, unroll=4)
+    def products(first, many, burg_z):
+        def row(k):
+            return pl.ds(8 * first + k, many, stride=8)
+
+        lx, ly, lz, bx, by = (ext[row(k), :] for k in (3, 4, 5, 6, 7))
+        sym[row(0), :] = 2.0 * bx * lx
+        sym[row(1), :] = 2.0 * by * ly
+        sym[row(2), :] = 2.0 * burg_z * lz
+        sym[row(3), :] = bx * ly + by * lx
+        sym[row(4), :] = bx * lz + burg_z * lx
+        sym[row(5), :] = by * lz + burg_z * ly
+        zero = jnp.zeros((many, LANES), F32)
+        sym[row(6), :] = zero
+        sym[row(7), :] = zero
+        ext[row(6), :] = lx * lx + ly * ly + lz * lz
+
+    for b in range(0, blocks, 8):
+        products(b, 8, bz[b : b + 8])
     for r in range(4):
-
-        def ghost_products(g, _):
-            base = pl.multiple_of((blocks + r * width + g) * 8, 8)
-            products(ghosts[r, at_block(g), :], base, ghosts[r, pl.ds(8 * width + g, 1), :])
-            return 0
-
-        lax.fori_loop(0, width, ghost_products, 0, unroll=4)
+        for g in range(0, width, 8):
+            products(blocks + r * width + g, 8, ghosts[r, 8 * width + g : 8 * width + g + 8])
 
     sub = lax.broadcasted_iota(jnp.int32, (8, LANES), 0)
     lane = lax.broadcasted_iota(jnp.int32, (8, LANES), 1)
     ahead = lane - sub
     scale = jnp.where(sub < 3, 0.5 * NEAR_COEF, jnp.where(sub < 6, NEAR_COEF, 0.0)).astype(F32)
     empty = jnp.zeros((8, LANES), F32)
-
-    def pair(p, _):
-        left = pairs[2 * p]
-        right = pairs[2 * p + 1]
-        floor = jnp.where(left == right, 0, -1024)
-        source = jnp.concatenate([ext[at_block(left), :], sym[at_block(left), :]], 0)
-        cols = source.T
-        tile_t = ext[at_block(right), :]
-        sym_t = sym[at_block(right), :]
-        a_high, a_low = split(cols)
-        b_high, b_low = split(jnp.concatenate([empty, sym_t * scale], 0))
-        dots = matmul(a_high, b_high) + (matmul(a_high, b_low) + matmul(a_low, b_high))
-        mt = [jnp.broadcast_to(tile_t[k : k + 1], (8, LANES)) for k in range(3)]
-        lt = [jnp.broadcast_to(tile_t[k + 3 : k + 4], (8, LANES)) for k in range(3)]
-        len_t = jnp.broadcast_to(sym_t[6:7], (8, LANES))
-        sums_t = [empty] * 6
-        columns = []
-        for c in range(LANES // 8):
-            col = cols[8 * c : 8 * c + 8]
-            ms = [col[:, k : k + 1] for k in range(3)]
-            ls = [col[:, k + 3 : k + 4] for k in range(3)]
-            len_s = col[:, 14:15]
-            rel = [mt[k] - ms[k] for k in range(3)]
-            quad = rel[0] * rel[0] + rel[1] * rel[1] + rel[2] * rel[2] + CORE_SQ
-            inv = lax.rsqrt(quad)
-            coef = dots[8 * c : 8 * c + 8] * (inv * inv * inv)
-            coef = jnp.where(ahead > floor + 8 * c, coef, 0.0)
-            push = [coef * rel[k] for k in range(3)]
-            along_s = ls[0] * rel[0] + ls[1] * rel[1] + ls[2] * rel[2]
-            along_t = lt[0] * rel[0] + lt[1] * rel[1] + lt[2] * rel[2]
-            den_s = quad + len_s
-            den_t = quad + len_t
-            both = den_s * den_t
-            near = pl.reciprocal(both, approx=True)
-            near = near * (2.0 - both * near)
-            half = 0.5 * near
-            share_s = along_s * den_t * half
-            share_t = along_t * den_s * half
-            skew_s = [share_s * push[k] for k in range(3)]
-            for k in range(3):
-                sums_t[k] = sums_t[k] + push[k]
-                sums_t[k + 3] = sums_t[k + 3] - share_t * push[k]
-            made = empty
-            for k, value in enumerate(push + skew_s):
-                made = jnp.where(lane == k, jnp.sum(value, 1, keepdims=True), made)
-            columns.append(made)
-        rows_s = jnp.concatenate(columns, 0).T[0:8]
-        acc[at_block(left), :] = acc[at_block(left), :] - rows_s
-        rows_t = empty
-        for k in range(6):
-            rows_t = jnp.where(sub == k, jnp.sum(sums_t[k], 0, keepdims=True), rows_t)
-        acc[at_block(right), :] = acc[at_block(right), :] + rows_t
-        return 0
-
-    lax.fori_loop(0, count[0], pair, 0)
+    listed = count[0]
+
+    def loop(body, at_once):
+        def several(q, _):
+            body([q * at_once + k for k in range(at_once)])
+            return 0
+
+        lax.fori_loop(0, (listed + 3) // 4 * (4 // at_once), several, 0)
+
+    def halves(value):
+        high, low = split(value)
+        return high.astype(F32), low.astype(F32)
+
+    def turn(group):
+        for p in group:
+            left, right = pairs[2 * p], pairs[2 * p + 1]
+            s_high, s_low = halves(sym[at_block(left), :])
+            t_high, t_low = halves(sym[at_block(right), :] * scale)
+            col = jnp.concatenate([ext[at_block(left), :], s_high, s_high, s_low], 0).T
+            other = jnp.concatenate([empty, t_high, t_low, t_high], 0)
+            cols[p, :, 0:32] = col
+            dots[p] = matmul(col.astype(BF16), other.astype(BF16))
+
+    def forces(group):
+        for p in group:
+            left, right = pairs[2 * p], pairs[2 * p + 1]
+            floor = jnp.where(left == right, 0, -1024)
+            floor = jnp.where(p < listed, floor, 1024)
+            tile_t = ext[at_block(right), :]
+            mt = [jnp.broadcast_to(tile_t[k : k + 1], (8, LANES)) for k in range(3)]
+            lt = [jnp.broadcast_to(tile_t[k + 3 : k + 4], (8, LANES)) for k in range(3)]
+            len_t = jnp.broadcast_to(tile_t[6:7], (8, LANES))
+            sums_t = [empty] * 6
+            for c in range(LANES // 8):
+                col = cols[p, 8 * c : 8 * c + 8, :]
+                ms = [col[:, k : k + 1] for k in range(3)]
+                ls = [col[:, k + 3 : k + 4] for k in range(3)]
+                len_s = col[:, 6:7]
+                rel = [mt[k] - ms[k] for k in range(3)]
+                quad = rel[0] * rel[0] + rel[1] * rel[1] + rel[2] * rel[2] + CORE_SQ
+                inv = lax.rsqrt(quad)
+                coef = dots[p, 8 * c : 8 * c + 8, :] * (inv * inv * inv)
+                coef = jnp.where(ahead > floor + 8 * c, coef, 0.0)
+                push = [coef * rel[k] for k in range(3)]
+                along_s = ls[0] * rel[0] + ls[1] * rel[1] + ls[2] * rel[2]
+                along_t = lt[0] * rel[0] + lt[1] * rel[1] + lt[2] * rel[2]
+                den_s = quad + len_s
+                den_t = quad + len_t
+                both = den_s * den_t
+                near = pl.reciprocal(both, approx=True)
+                near = near * (2.0 - both * near)
+                half = 0.5 * near
+                share_s = along_s * den_t * half
+                share_t = along_t * den_s * half
+                skew_s = [share_s * push[k] for k in range(3)]
+                for k in range(3):
+                    sums_t[k] = sums_t[k] + push[k]
+                    sums_t[k + 3] = sums_t[k + 3] - share_t * push[k]
+                wide = empty
+                for k, value in enumerate(push + skew_s):
+                    wide = jnp.where(lane == k, jnp.sum(value, 1, keepdims=True), wide)
+                made[p, 8 * c : 8 * c + 8, :] = wide
+            rows_t = empty
+            for k in range(6):
+                rows_t = jnp.where(sub == k, jnp.sum(sums_t[k], 0, keepdims=True), rows_t)
+            made[p, LANES : LANES + 8, :] = rows_t
+
+    def collect(group):
+        rows_s = [made[p, 0:LANES, :].T[0:8] for p in group]
+        rows_t = [made[p, LANES : LANES + 8, :] for p in group]
+        for k, p in enumerate(group):
+            left, right = pairs[2 * p], pairs[2 * p + 1]
+            acc[at_block(left), :] = acc[at_block(left), :] - rows_s[k]
+            acc[at_block(right), :] = acc[at_block(right), :] + rows_t[k]
+
+    loop(turn, 4)
+    loop(forces, 2)
+    loop(collect, 4)
 
     per_x = CELL_XY * CELL_Z
     groups = per_x // 8
@@ -309,11 +331,12 @@
     kys = [sub // CELL_Z + (8 // CELL_Z) * j for j in range(groups)]
     z_centre = (kz.astype(F32) + 0.5) / (16 * CELL_Z)
     y_centres = [(ky.astype(F32) + 0.5) / CELL_XY for ky in kys]
-    m_high, m_low = split(moments[...].T)
+    m_high, m_low = split(moments[...])
+    m_cols = jnp.concatenate([m_high.astype(F32), m_high.astype(F32), m_low.astype(F32)], 0).T.astype(BF16)
 
     def far(b, _):
         t_high, t_low = split(terms[:, at_lanes(b)])
-        weight = matmul(m_high, t_high) + (matmul(m_high, t_low) + matmul(m_low, t_high))
+        weight = matmul(m_cols, jnp.concatenate([t_high, t_low, t_high], 0))
         tile = main[at_block(b), :]
         mx, my, mz = (jnp.broadcast_to(tile[k : k + 1], (8, LANES)) for k in range(3))
         here = jnp.broadcast_to(cell[pl.ds(b, 1), :], (8, LANES))
@@ -348,7 +371,7 @@
         own_acc[at_block(b), :] = acc[at_block(b), :] + FAR_COEF * rows
         return 0
 
-    lax.fori_loop(0, blocks, far, 0)
+    lax.fori_loop(0, blocks, far, 0, unroll=4)
     for r in range(4):
         lo = 8 * (blocks + r * width)
         ghost_acc[r] = acc[lo : lo + 8 * width]
@@ -385,6 +408,7 @@
     blocks = seg_here // LANES
     width = send_blocks.shape[2]
     sent_rows = 9 * width
+    most = pair_list.shape[1]
     (ax, nx), (ay, ny) = sizes
     slots = send_blocks.reshape(-1)
     counts = send_count.reshape(-1)
@@ -436,7 +460,9 @@
         out_shape=(shape(blocks * 8, LANES), shape(4, 8 * width, LANES)),
         in_specs=[SMEM_SPEC] * 2 + [VMEM_SPEC] * 6,
         out_specs=(VMEM_SPEC,) * 2,
-        scratch_shapes=[pltpu.VMEM(((blocks + 4 * width) * 8, LANES), F32)] * 3,
+        scratch_shapes=[pltpu.VMEM(((blocks + 4 * width) * 8, LANES), F32)] * 3
+        + [pltpu.VMEM((most, LANES, LANES), F32)] * 2
+        + [pltpu.VMEM((most, LANES + 8, LANES), F32)],
         compiler_params=params,
         name="interact",
     )(pair_list.reshape(-1), count, main, bz, ghosts, cell, terms, moments)

time: 132 us -> 140 us (1.061)
  Pallas kernels: 126 us -> 135 us
    pallas_call x1, Pallas kernels: 50.6 us -> 113 us  [on_device(): pl.pallas_call(functools.partial(interact, width), out_shape=(shape(block...]
    pallas_call x1, Pallas kernels: 57.5 us -> 4.75 us  [on_device(): pl.pallas_call(functools.partial(give_back, sizes), out_shape=shape(4, 8...]
where the time goes in v2:
time: 140 us
  Pallas kernels  135 us (96%)
  local copies, waits for them, and re-layouts  5.21 us (4%)
    pallas_call x1, Pallas kernels, on_device(): pl.pallas_call(functools.partial(interact, width), out_shape=(shape(block...  113 us
    pallas_call x1, Pallas kernels, on_device(): pl.pallas_call(functools.partial(exchange, sizes), out_shape=(shape(4, se...  12.4 us
    pallas_call x1, Pallas kernels, on_device(): pl.pallas_call(functools.partial(give_back, sizes), out_shape=shape(4, 8...  4.75 us
    unnamed x15, local copies, waits for them, and re-layouts  4.41 us
    pallas_call x1, Pallas kernels, on_device(): pl.pallas_call(functools.partial(prepare, width), out_shape=(shape(blocks...  3.35 us

profile of v2, /device:TPU:0, one launch (start us, length us, event | category | flops | bytes accessed | tf_op | source)
XLA Modules:
  0.0 140.4 jit_solution(16001691155568245377)
XLA Ops:
  0.0 0.0 copy-start.6
  0.0 0.7 copy-done.6
  0.7 0.6 dynamic_slice.3.count
  1.2 0.0 copy-start.4
  1.2 0.7 copy-done.4
  1.9 0.0 copy-start.5
  1.9 0.1 reshape.12.slots
  2.0 0.6 copy-done.5
  2.6 0.0 copy-start.2
  2.6 0.1 copy.9
  2.7 0.0 copy-start.3
  2.7 0.1 reshape.14.pairs
  2.8 0.5 copy-done.2
  3.4 0.0 copy-done.3
  3.4 0.0 copy-start
  3.4 0.9 copy-done
  4.3 0.0 copy-start.1
  4.3 0.9 copy-done.1
  5.2 3.4 %prepare.1 = (f32[512,128]{1,0:T(8,128)S(1)}, f32[64,128]{1,0:T(8,128)S(1)}, f32[16,8192]{1,0:T(8,128)S(1)}, f32[4,216,128]{2,1,0:T(8,128)S(1)}, f32[16,256]{1,0:T(8,128)S(1)}) custom-call(s32[96]{0:T(128)S(1)} %reshape.12.slots, s32[4]{0:T(128)S(1)} %bitcast.4, f32[6,8192]{1,0:T(8,128)S(1)} %copy-done, f32[3,8192]{1,0:T(4,128)S(1)} %copy-done.1, ...), custom_call_target="tpu_custom_call" | custom-call | tf_op jit(solution)/shard_map/prepare/pallas_call | solution.py:420
  8.6 12.4 %exchange.1 = (f32[4,216,128]{2,1,0:T(8,128)S(1)}, f32[16,256]{1,0:T(8,128)S(1)}) custom-call(f32[4,216,128]{2,1,0:T(8,128)S(1)} %get-tuple-element.16.outgoing, f32[16,256]{1,0:T(8,128)S(1)} %get-tuple-element.17.local), custom_call_target="tpu_custom_call" | custom-call | tf_op jit(solution)/shard_map/exchange/pallas_call | solution.py:436
  20.9 112.7 %interact.1 = (f32[512,128]{1,0:T(8,128)S(1)}, f32[4,192,128]{2,1,0:T(8,128)S(1)}) custom-call(s32[128]{0:T(128)S(1)} %reshape.14.pairs, s32[1]{0:T(128)} %dynamic_slice.3.count, f32[512,128]{1,0:T(8,128)S(1)} %get-tuple-element.14.main, f32[64,128]{1,0:T(8,128)S(1)} %get-tuple-element.15.bz, f32[4,216,128]{2,1,0:T(8,128)S(1)} %get-tuple-element.18.ghosts, ...), custom_call_target="tpu_custom_call" | custom-call | tf_op jit(solution)/shard_map/interact/pallas_call | solution.py:458
  133.7 4.8 %give_back.1.returned = f32[4,192,128]{2,1,0:T(8,128)S(1)} custom-call(f32[4,192,128]{2,1,0:T(8,128)S(1)} %get-tuple-element.22.forces), custom_call_target="tpu_custom_call" | custom-call | tf_op jit(solution)/shard_map/give_back/pallas_call | solution.py:470
  138.4 1.9 %finish.1 = f32[6,8192]{1,0:T(8,128)} custom-call(s32[96]{0:T(128)S(1)} %reshape.12.slots, s32[4]{0:T(128)S(1)} %bitcast.5, f32[512,128]{1,0:T(8,128)S(1)} %get-tuple-element.21.own_acc, f32[4,192,128]{2,1,0:T(8,128)S(1)} %give_back.1.returned), custom_call_target="tpu_custom_call" | custom-call | tf_op jit(solution)/shard_map/finish/pallas_call | solution.py:482
Async XLA Ops:
  0.0 0.7 copy-start.6
  1.2 0.7 copy-start.4
  1.9 0.7 copy-start.5
  2.6 0.8 copy-start.2
  2.7 0.7 copy-start.3
  3.4 1.0 copy-start
  4.3 0.9 copy-start.1

commit v3 on v1

--- a/solution.py
+++ b/solution.py
@@ -13,6 +13,7 @@
 LANES = 128
 TERM_ROWS = 16
 CHUNK = 1024
+AT_ONCE = 2
 
 CORE_SQ = 2.5e-05
 NEAR_COEF = 0.2
@@ -208,7 +209,9 @@
     wait_all(copies)
 
 
-def interact(width, pairs, count, main, bz, ghosts, cell, terms, moments, own_acc, ghost_acc, ext, sym, acc):
+def interact(
+    width, pairs, count, main, bz, ghosts, cell, terms, moments, own_acc, ghost_acc, ext, sym, acc, rhs, wide, xs
+):
     blocks = main.shape[0] // 8
     total = blocks + 4 * width
     acc[...] = jnp.zeros_like(acc)
@@ -217,63 +220,89 @@
         lo = 8 * (blocks + r * width)
         ext[lo : lo + 8 * width] = ghosts[r, 0 : 8 * width]
 
-    def products(tile, base, burg_z):
-        lx, ly, lz, bx, by = (tile[k : k + 1] for k in (3, 4, 5, 6, 7))
-        sym[pl.ds(base, 1), :] = 2.0 * bx * lx
-        sym[pl.ds(base + 1, 1), :] = 2.0 * by * ly
-        sym[pl.ds(base + 2, 1), :] = 2.0 * burg_z * lz
-        sym[pl.ds(base + 3, 1), :] = bx * ly + by * lx
-        sym[pl.ds(base + 4, 1), :] = bx * lz + burg_z * lx
-        sym[pl.ds(base + 5, 1), :] = by * lz + burg_z * ly
-        sym[pl.ds(base + 6, 1), :] = lx * lx + ly * ly + lz * lz
-        sym[pl.ds(base + 7, 1), :] = jnp.zeros((1, LANES), F32)
-
-    def own_products(b, _):
-        products(main[at_block(b), :], pl.multiple_of(b * 8, 8), bz[pl.ds(b, 1), :])
-        return 0
-
-    lax.fori_loop(0, blocks, own_products, 0, unroll=4)
+    def products(first, many, burg_z):
+        def row(k):
+            return pl.ds(8 * first + k, many, stride=8)
+
+        lx, ly, lz, bx, by = (ext[row(k), :] for k in (3, 4, 5, 6, 7))
+        sym[row(0), :] = 2.0 * bx * lx
+        sym[row(1), :] = 2.0 * by * ly
+        sym[row(2), :] = 2.0 * burg_z * lz
+        sym[row(3), :] = bx * ly + by * lx
+        sym[row(4), :] = bx * lz + burg_z * lx
+        sym[row(5), :] = by * lz + burg_z * ly
+        zero = jnp.zeros((many, LANES), F32)
+        sym[row(6), :] = zero
+        sym[row(7), :] = zero
+        ext[row(6), :] = lx * lx + ly * ly + lz * lz
+
+    for b in range(0, blocks, 8):
+        products(b, 8, bz[b : b + 8])
     for r in range(4):
-
-        def ghost_products(g, _):
-            base = pl.multiple_of((blocks + r * width + g) * 8, 8)
-            products(ghosts[r, at_block(g), :], base, ghosts[r, pl.ds(8 * width + g, 1), :])
-            return 0
-
-        lax.fori_loop(0, width, ghost_products, 0, unroll=4)
+        for g in range(0, width, 8):
+            products(blocks + r * width + g, 8, ghosts[r, 8 * width + g : 8 * width + g + 8])
 
     sub = lax.broadcasted_iota(jnp.int32, (8, LANES), 0)
-    lane = lax.broadcasted_iota(jnp.int32, (8, LANES), 1)
-    ahead = lane - sub
+    ahead = lax.broadcasted_iota(jnp.int32, (16, LANES), 1) - lax.broadcasted_iota(jnp.int32, (16, LANES), 0)
     scale = jnp.where(sub < 3, 0.5 * NEAR_COEF, jnp.where(sub < 6, NEAR_COEF, 0.0)).astype(F32)
     empty = jnp.zeros((8, LANES), F32)
-
-    def pair(p, _):
-        left = pairs[2 * p]
-        right = pairs[2 * p + 1]
+    listed = count[0]
+
+    def parts(value, many):
+        out = []
+        for _ in range(many):
+            part = value.astype(BF16).astype(F32)
+            out.append(part)
+            value = value - part
+        return out
+
+    depth, across = rhs.shape[1:]
+    row = lax.broadcasted_iota(jnp.int32, (depth, across), 0)
+    out_id = lax.broadcasted_iota(jnp.int32, (depth, across), 1) // LANES - 1
+    pick = jnp.where(out_id < 3, -1.0, 1.0)
+    pattern = jnp.where(jnp.logical_and(row < 24, row % 8 == out_id), pick, 0.0).astype(BF16)
+    for slot in range(AT_ONCE):
+        rhs[slot] = pattern
+    ones = jnp.ones((8, LANES), F32)
+    edge = [jnp.where(sub == k, -1.0, 0.0).astype(F32) for k in range(3)]
+    summed = xs.shape[2]
+    adder = jnp.where(
+        lax.broadcasted_iota(jnp.int32, (8, summed), 1) // (2 * LANES)
+        == lax.broadcasted_iota(jnp.int32, (8, summed), 0),
+        1.0,
+        0.0,
+    ).astype(BF16)
+
+    def turn(slot, p):
+        left, right = pairs[2 * p], pairs[2 * p + 1]
+        s_high, s_low = parts(sym[at_block(left), :], 2)
+        t_high, t_low = parts(sym[at_block(right), :] * scale, 2)
+        own = parts(ext[at_block(left), :], 3)
+        other = parts(ext[at_block(right), :], 3)
+        col = jnp.concatenate(own + [ones] * 3 + [s_high, s_high, s_low, empty], 0).T
+        rhs[slot, 48:80, 0:LANES] = jnp.concatenate([t_high, t_low, t_high, empty], 0).astype(BF16)
+        for k in range(3):
+            keep = jnp.where(sub == k, 1.0, 0.0)
+            rows = jnp.concatenate([edge[k]] + [part * keep for part in other], 0)
+            rhs[slot, 16:48, (k + 1) * LANES : (k + 2) * LANES] = rows.astype(BF16)
+        wide[slot] = matmul(col.astype(BF16), rhs[slot])
+
+    def forces(slot, p):
+        left, right = pairs[2 * p], pairs[2 * p + 1]
         floor = jnp.where(left == right, 0, -1024)
-        source = jnp.concatenate([ext[at_block(left), :], sym[at_block(left), :]], 0)
-        cols = source.T
+        floor = jnp.where(p < listed, floor, 1024)
         tile_t = ext[at_block(right), :]
-        sym_t = sym[at_block(right), :]
-        a_high, a_low = split(cols)
-        b_high, b_low = split(jnp.concatenate([empty, sym_t * scale], 0))
-        dots = matmul(a_high, b_high) + (matmul(a_high, b_low) + matmul(a_low, b_high))
-        mt = [jnp.broadcast_to(tile_t[k : k + 1], (8, LANES)) for k in range(3)]
-        lt = [jnp.broadcast_to(tile_t[k + 3 : k + 4], (8, LANES)) for k in range(3)]
-        len_t = jnp.broadcast_to(sym_t[6:7], (8, LANES))
-        sums_t = [empty] * 6
-        columns = []
-        for c in range(LANES // 8):
-            col = cols[8 * c : 8 * c + 8]
-            ms = [col[:, k : k + 1] for k in range(3)]
-            ls = [col[:, k + 3 : k + 4] for k in range(3)]
-            len_s = col[:, 14:15]
-            rel = [mt[k] - ms[k] for k in range(3)]
+        lt = [tile_t[k + 3 : k + 4] for k in range(3)]
+        len_t = tile_t[6:7]
+        sums_t = [jnp.zeros((8, LANES), F32)] * 6
+        for c in range(LANES // 16):
+            lo = 16 * c
+            known = [wide[slot, lo : lo + 16, k * LANES : (k + 1) * LANES] for k in range(8)]
+            rel, ls, len_s = known[1:4], known[4:7], known[7]
             quad = rel[0] * rel[0] + rel[1] * rel[1] + rel[2] * rel[2] + CORE_SQ
             inv = lax.rsqrt(quad)
-            coef = dots[8 * c : 8 * c + 8] * (inv * inv * inv)
-            coef = jnp.where(ahead > floor + 8 * c, coef, 0.0)
+            coef = known[0] * (inv * inv * inv)
+            coef = jnp.where(ahead > floor + lo, coef, 0.0)
             push = [coef * rel[k] for k in range(3)]
             along_s = ls[0] * rel[0] + ls[1] * rel[1] + ls[2] * rel[2]
             along_t = lt[0] * rel[0] + lt[1] * rel[1] + lt[2] * rel[2]
@@ -285,23 +314,32 @@
             half = 0.5 * near
             share_s = along_s * den_t * half
             share_t = along_t * den_s * half
-            skew_s = [share_s * push[k] for k in range(3)]
             for k in range(3):
-                sums_t[k] = sums_t[k] + push[k]
-                sums_t[k + 3] = sums_t[k + 3] - share_t * push[k]
-            made = empty
-            for k, value in enumerate(push + skew_s):
-                made = jnp.where(lane == k, jnp.sum(value, 1, keepdims=True), made)
-            columns.append(made)
-        rows_s = jnp.concatenate(columns, 0).T[0:8]
-        acc[at_block(left), :] = acc[at_block(left), :] - rows_s
+                skew = share_t * push[k]
+                sums_t[k] = sums_t[k] + (push[k][0:8] + push[k][8:16])
+                sums_t[k + 3] = sums_t[k + 3] - (skew[0:8] + skew[8:16])
+            for k, value in enumerate(push + [share_s * push[k] for k in range(3)]):
+                high, low = split(value)
+                xs[slot, lo : lo + 16, 2 * k * LANES : (2 * k + 1) * LANES] = high
+                xs[slot, lo : lo + 16, (2 * k + 1) * LANES : (2 * k + 2) * LANES] = low
         rows_t = empty
         for k in range(6):
             rows_t = jnp.where(sub == k, jnp.sum(sums_t[k], 0, keepdims=True), rows_t)
-        acc[at_block(right), :] = acc[at_block(right), :] + rows_t
+        rows_s = lax.dot_general(adder, xs[slot], (((1,), (1,)), ((), ())), preferred_element_type=F32)
+        return rows_s, rows_t
+
+    def several(q, _):
+        group = [(slot, q * AT_ONCE + slot) for slot in range(AT_ONCE)]
+        for slot, p in group:
+            turn(slot, p)
+        rows = [forces(slot, p) for slot, p in group]
+        for slot, p in group:
+            left, right = pairs[2 * p], pairs[2 * p + 1]
+            acc[at_block(left), :] = acc[at_block(left), :] - rows[slot][0]
+            acc[at_block(right), :] = acc[at_block(right), :] + rows[slot][1]
         return 0
 
-    lax.fori_loop(0, count[0], pair, 0)
+    lax.fori_loop(0, (listed + AT_ONCE - 1) // AT_ONCE, several, 0)
 
     per_x = CELL_XY * CELL_Z
     groups = per_x // 8
@@ -309,11 +347,12 @@
     kys = [sub // CELL_Z + (8 // CELL_Z) * j for j in range(groups)]
     z_centre = (kz.astype(F32) + 0.5) / (16 * CELL_Z)
     y_centres = [(ky.astype(F32) + 0.5) / CELL_XY for ky in kys]
-    m_high, m_low = split(moments[...].T)
+    m_high, m_low = split(moments[...])
+    m_cols = jnp.concatenate([m_high.astype(F32), m_high.astype(F32), m_low.astype(F32)], 0).T.astype(BF16)
 
     def far(b, _):
         t_high, t_low = split(terms[:, at_lanes(b)])
-        weight = matmul(m_high, t_high) + (matmul(m_high, t_low) + matmul(m_low, t_high))
+        weight = matmul(m_cols, jnp.concatenate([t_high, t_low, t_high], 0))
         tile = main[at_block(b), :]
         mx, my, mz = (jnp.broadcast_to(tile[k : k + 1], (8, LANES)) for k in range(3))
         here = jnp.broadcast_to(cell[pl.ds(b, 1), :], (8, LANES))
@@ -348,7 +387,7 @@
         own_acc[at_block(b), :] = acc[at_block(b), :] + FAR_COEF * rows
         return 0
 
-    lax.fori_loop(0, blocks, far, 0)
+    lax.fori_loop(0, blocks, far, 0, unroll=4)
     for r in range(4):
         lo = 8 * (blocks + r * width)
         ghost_acc[r] = acc[lo : lo + 8 * width]
@@ -436,7 +475,12 @@
         out_shape=(shape(blocks * 8, LANES), shape(4, 8 * width, LANES)),
         in_specs=[SMEM_SPEC] * 2 + [VMEM_SPEC] * 6,
         out_specs=(VMEM_SPEC,) * 2,
-        scratch_shapes=[pltpu.VMEM(((blocks + 4 * width) * 8, LANES), F32)] * 3,
+        scratch_shapes=[pltpu.VMEM(((blocks + 4 * width) * 8, LANES), F32)] * 3
+        + [
+            pltpu.VMEM((AT_ONCE, 80, 8 * LANES), BF16),
+            pltpu.VMEM((AT_ONCE, LANES, 8 * LANES), F32),
+            pltpu.VMEM((AT_ONCE, LANES, 12 * LANES), BF16),
+        ],
         compiler_params=params,
         name="interact",
     )(pair_list.reshape(-1), count, main, bz, ghosts, cell, terms, moments)

time: 132 us -> 58.7 us (0.44)
  Pallas kernels: 126 us -> 53.3 us
    pallas_call x1, Pallas kernels: 57.5 us -> 20.9 us  [on_device(): pl.pallas_call(functools.partial(give_back, sizes), out_shape=shape(4, 8...]
    pallas_call x1, Pallas kernels: 50.6 us -> 14.9 us  [on_device(): pl.pallas_call(functools.partial(interact, width), out_shape=(shape(block...]
where the time goes in v3:
time: 58.7 us; the launch traced here: 58.6 us
  Pallas kernels  53.3 us (91%)
  local copies, waits for them, and re-layouts  5.21 us (9%)
    pallas_call x1, Pallas kernels, on_device(): pl.pallas_call(functools.partial(give_back, sizes), out_shape=shape(4, 8...  20.9 us
    pallas_call x1, Pallas kernels, on_device(): pl.pallas_call(functools.partial(interact, width), out_shape=(shape(block...  14.9 us
    pallas_call x1, Pallas kernels, on_device(): pl.pallas_call(functools.partial(exchange, sizes), out_shape=(shape(4, se...  12.4 us
    unnamed x15, local copies, waits for them, and re-layouts  4.41 us
    pallas_call x1, Pallas kernels, on_device(): pl.pallas_call(functools.partial(prepare, width), out_shape=(shape(blocks...  3.35 us
    pallas_call x1, Pallas kernels, on_device(): pl.pallas_call(functools.partial(finish, width), out_shape=shape(6, seg_h...  1.86 us

profile of v3, /device:TPU:0, one launch (start us, length us, event | category | flops | bytes accessed | tf_op | source)
XLA Modules:
  0.0 58.6 jit_solution(10253708526234201148)
XLA Ops:
  0.0 0.0 copy-start.6
  0.0 0.7 %copy-done.6 = s32[32]{0:T(128)S(1)} copy-done((s32[32]{0:T(128)S(1)}, s32[32]{0:T(128)}, u32[]{:S(2)}) %copy-start.6) | copy-done | bytes 152
  0.7 0.6 dynamic_slice.3.count
  1.2 0.0 copy-start.4
  1.2 0.7 %copy-done.4 = s32[1,4,24]{2,1,0:T(4,128)S(1)} copy-done((s32[1,4,24]{2,1,0:T(4,128)S(1)}, s32[1,4,24]{2,1,0:T(4,128)}, u32[]{:S(2)}) %copy-start.4) | copy-done | bytes 408
  1.9 0.0 copy-start.5
  1.9 0.1 reshape.12.slots
  2.0 0.6 %copy-done.5 = s32[1,64,2]{1,2,0:T(2,128)S(1)} copy-done((s32[1,64,2]{1,2,0:T(2,128)S(1)}, s32[1,64,2]{1,2,0:T(2,128)}, u32[]{:S(2)}) %copy-start.5) | copy-done | bytes 536
  2.6 0.0 copy-start.2
  2.6 0.1 copy.9
  2.7 0.0 copy-start.3
  2.7 0.1 reshape.14.pairs
  2.8 0.5 copy-done.2
  3.4 0.0 copy-done.3
  3.4 0.0 copy-start
  3.4 0.9 %copy-done = f32[6,8192]{1,0:T(8,128)S(1)} copy-done((f32[6,8192]{1,0:T(8,128)S(1)}, f32[6,8192]{1,0:T(8,128)}, u32[]{:S(2)}) %copy-start) | copy-done | bytes 196632
  4.3 0.0 copy-start.1
  4.3 0.9 %copy-done.1 = f32[3,8192]{1,0:T(4,128)S(1)} copy-done((f32[3,8192]{1,0:T(4,128)S(1)}, f32[3,8192]{1,0:T(4,128)}, u32[]{:S(2)}) %copy-start.1) | copy-done | bytes 98328
  5.2 3.4 %prepare.1 = (f32[512,128]{1,0:T(8,128)S(1)}, f32[64,128]{1,0:T(8,128)S(1)}, f32[16,8192]{1,0:T(8,128)S(1)}, f32[4,216,128]{2,1,0:T(8,128)S(1)}, f32[16,256]{1,0:T(8,128)S(1)}) custom-call(s32[96]{0:T(128)S(1)} %reshape.12.slots, s32[4]{0:T(128)S(1)} %bitcast.4, f32[6,8192]{1,0:T(8,128)S(1)} %copy-done, f32[3,8192]{1,0:T(4,128)S(1)} %copy-done.1, ...), custom_call_target="tpu_custom_call" | custom-call | tf_op jit(solution)/shard_map/prepare/pallas_call | solution.py:435
  8.6 12.4 %exchange.1 = (f32[4,216,128]{2,1,0:T(8,128)S(1)}, f32[16,256]{1,0:T(8,128)S(1)}) custom-call(f32[4,216,128]{2,1,0:T(8,128)S(1)} %get-tuple-element.16.outgoing, f32[16,256]{1,0:T(8,128)S(1)} %get-tuple-element.17.local), custom_call_target="tpu_custom_call" | custom-call | tf_op jit(solution)/shard_map/exchange/pallas_call | solution.py:451
  20.9 14.9 %interact.1 = (f32[512,128]{1,0:T(8,128)S(1)}, f32[4,192,128]{2,1,0:T(8,128)S(1)}) custom-call(s32[128]{0:T(128)S(1)} %reshape.14.pairs, s32[1]{0:T(128)} %dynamic_slice.3.count, f32[512,128]{1,0:T(8,128)S(1)} %get-tuple-element.14.main, f32[64,128]{1,0:T(8,128)S(1)} %get-tuple-element.15.bz, f32[4,216,128]{2,1,0:T(8,128)S(1)} %get-tuple-element.18.ghosts, ...), custom_call_target="tpu_custom_call" | custom-call | tf_op jit(solution)/shard_map/interact/pallas_call | solution.py:473
  35.8 20.9 %give_back.1.returned = f32[4,192,128]{2,1,0:T(8,128)S(1)} custom-call(f32[4,192,128]{2,1,0:T(8,128)S(1)} %get-tuple-element.22.forces), custom_call_target="tpu_custom_call" | custom-call | tf_op jit(solution)/shard_map/give_back/pallas_call | solution.py:488
  56.7 1.9 %finish.1 = f32[6,8192]{1,0:T(8,128)} custom-call(s32[96]{0:T(128)S(1)} %reshape.12.slots, s32[4]{0:T(128)S(1)} %bitcast.5, f32[512,128]{1,0:T(8,128)S(1)} %get-tuple-element.21.own_acc, f32[4,192,128]{2,1,0:T(8,128)S(1)} %give_back.1.returned), custom_call_target="tpu_custom_call" | custom-call | tf_op jit(solution)/shard_map/finish/pallas_call | solution.py:500
Async XLA Ops:
  0.0 0.7 %copy-start.6 = (s32[32]{0:T(128)S(1)}, s32[32]{0:T(128)}, u32[]{:S(2)}) copy-start(s32[32]{0:T(128)} %param.13) | copy-start | bytes 388
  1.2 0.7 %copy-start.4 = (s32[1,4,24]{2,1,0:T(4,128)S(1)}, s32[1,4,24]{2,1,0:T(4,128)}, u32[]{:S(2)}) copy-start(s32[1,4,24]{2,1,0:T(4,128)} %param.10) | copy-start | bytes 1156
  1.9 0.7 %copy-start.5 = (s32[1,64,2]{1,2,0:T(2,128)S(1)}, s32[1,64,2]{1,2,0:T(2,128)}, u32[]{:S(2)}) copy-start(s32[1,64,2]{1,2,0:T(2,128)} %param.12) | copy-start | bytes 1540
  2.6 0.8 %copy-start.2 = (s32[8192]{0:T(1024)S(1)}, s32[8192]{0:T(1024)}, u32[]{:S(2)}) copy-start(s32[8192]{0:T(1024)} %param.9) | copy-start | bytes 98308
  2.7 0.7 %copy-start.3 = (s32[1,4]{1,0:T(1,128)S(1)}, s32[1,4]{1,0:T(1,128)}, u32[]{:S(2)}) copy-start(s32[1,4]{1,0:T(1,128)} %param.11) | copy-start | bytes 52
  3.4 1.0 %copy-start = (f32[6,8192]{1,0:T(8,128)S(1)}, f32[6,8192]{1,0:T(8,128)}, u32[]{:S(2)}) copy-start(f32[6,8192]{1,0:T(8,128)} %ends.1) | copy-start | bytes 589828
  4.3 0.9 %copy-start.1 = (f32[3,8192]{1,0:T(4,128)S(1)}, f32[3,8192]{1,0:T(4,128)}, u32[]{:S(2)}) copy-start(f32[3,8192]{1,0:T(4,128)} %burgers.1) | copy-start | bytes 294916

commit v4 on v3

--- a/solution.py
+++ b/solution.py
@@ -13,7 +13,7 @@
 LANES = 128
 TERM_ROWS = 16
 CHUNK = 1024
-AT_ONCE = 2
+AT_ONCE = 4
 
 CORE_SQ = 2.5e-05
 NEAR_COEF = 0.2
@@ -202,15 +202,69 @@
     wait_all(copies)
 
 
-def give_back(sizes, forces, returned, send_sem, recv_sem):
+def far_forces(main, cell, terms, moments, forces):
+    blocks = main.shape[0] // 8
+    sub = lax.broadcasted_iota(jnp.int32, (8, LANES), 0)
+    empty = jnp.zeros((8, LANES), F32)
+    per_x = CELL_XY * CELL_Z
+    groups = per_x // 8
+    kz = sub % CELL_Z
+    kys = [sub // CELL_Z + (8 // CELL_Z) * j for j in range(groups)]
+    z_centre = (kz.astype(F32) + 0.5) / (16 * CELL_Z)
+    y_centres = [(ky.astype(F32) + 0.5) / CELL_XY for ky in kys]
+    m_high, m_low = split(moments[...])
+    m_cols = jnp.concatenate([m_high.astype(F32), m_high.astype(F32), m_low.astype(F32)], 0).T.astype(BF16)
+
+    def far(b, _):
+        t_high, t_low = split(terms[:, at_lanes(b)])
+        weight = matmul(m_cols, jnp.concatenate([t_high, t_low, t_high], 0))
+        tile = main[at_block(b), :]
+        mx, my, mz = (jnp.broadcast_to(tile[k : k + 1], (8, LANES)) for k in range(3))
+        here = jnp.broadcast_to(cell[pl.ds(b, 1), :], (8, LANES))
+        cx, cy, cz = here // per_x, here // CELL_Z % CELL_XY, here % CELL_Z
+        rz = z_centre - mz
+        rys = [centre - my for centre in y_centres]
+        flat = [ry * ry + rz * rz + CORE_SQ for ry in rys]
+        gap_z = jnp.abs(kz - cz)
+        gaps = [jnp.maximum(jnp.abs(ky - cy), gap_z) for ky in kys]
+        sums = [empty] * groups
+        fx = empty
+        for kx in range(CELL_XY):
+            rx = (kx + 0.5) / CELL_XY - mx
+            square = rx * rx
+            gap_x = jnp.abs(cx - kx)
+            plane = empty
+            for j in range(groups):
+                inv = lax.rsqrt(square + flat[j])
+                lo = kx * per_x + 8 * j
+                coef = weight[lo : lo + 8] * (inv * inv * inv)
+                coef = jnp.where(jnp.maximum(gap_x, gaps[j]) >= 2, coef, 0.0)
+                sums[j] = sums[j] + coef
+                plane = plane + coef
+            fx = fx + rx * plane
+        fy, fall = empty, empty
+        for j in range(groups):
+            fy = fy + rys[j] * sums[j]
+            fall = fall + sums[j]
+        rows = empty
+        for k, value in enumerate((fx, fy, rz * fall)):
+            rows = jnp.where(sub == k, jnp.sum(value, 0, keepdims=True), rows)
+        forces[at_block(b), :] = FAR_COEF * rows
+        return 0
+
+    lax.fori_loop(0, blocks, far, 0, unroll=4)
+
+
+def give_back(sizes, forces, main, cell, terms, moments, returned, far, send_sem, recv_sem):
     hello_near(sizes)
     copies = neighbours(sizes, forces, returned, send_sem, recv_sem)
     start_all(copies, returned)
+    far_forces(main, cell, terms, moments, far)
     wait_all(copies)
 
 
 def interact(
-    width, pairs, count, main, bz, ghosts, cell, terms, moments, own_acc, ghost_acc, ext, sym, acc, rhs, wide, xs
+    sizes, width, pairs, counts, main, bz, ghosts, own_acc, ghost_acc, ext, sym, acc, rhs, wide, xs
 ):
     blocks = main.shape[0] // 8
     total = blocks + 4 * width
@@ -246,7 +300,8 @@
     ahead = lax.broadcasted_iota(jnp.int32, (16, LANES), 1) - lax.broadcasted_iota(jnp.int32, (16, LANES), 0)
     scale = jnp.where(sub < 3, 0.5 * NEAR_COEF, jnp.where(sub < 6, NEAR_COEF, 0.0)).astype(F32)
     empty = jnp.zeros((8, LANES), F32)
-    listed = count[0]
+    (ax, _), (ay, ny) = sizes
+    listed = counts[lax.axis_index(ax) * ny + lax.axis_index(ay)]
 
     def parts(value, many):
         out = []
@@ -341,61 +396,15 @@
 
     lax.fori_loop(0, (listed + AT_ONCE - 1) // AT_ONCE, several, 0)
 
-    per_x = CELL_XY * CELL_Z
-    groups = per_x // 8
-    kz = sub % CELL_Z
-    kys = [sub // CELL_Z + (8 // CELL_Z) * j for j in range(groups)]
-    z_centre = (kz.astype(F32) + 0.5) / (16 * CELL_Z)
-    y_centres = [(ky.astype(F32) + 0.5) / CELL_XY for ky in kys]
-    m_high, m_low = split(moments[...])
-    m_cols = jnp.concatenate([m_high.astype(F32), m_high.astype(F32), m_low.astype(F32)], 0).T.astype(BF16)
-
-    def far(b, _):
-        t_high, t_low = split(terms[:, at_lanes(b)])
-        weight = matmul(m_cols, jnp.concatenate([t_high, t_low, t_high], 0))
-        tile = main[at_block(b), :]
-        mx, my, mz = (jnp.broadcast_to(tile[k : k + 1], (8, LANES)) for k in range(3))
-        here = jnp.broadcast_to(cell[pl.ds(b, 1), :], (8, LANES))
-        cx, cy, cz = here // per_x, here // CELL_Z % CELL_XY, here % CELL_Z
-        rz = z_centre - mz
-        rys = [centre - my for centre in y_centres]
-        flat = [ry * ry + rz * rz + CORE_SQ for ry in rys]
-        gap_z = jnp.abs(kz - cz)
-        gaps = [jnp.maximum(jnp.abs(ky - cy), gap_z) for ky in kys]
-        sums = [empty] * groups
-        fx = empty
-        for kx in range(CELL_XY):
-            rx = (kx + 0.5) / CELL_XY - mx
-            square = rx * rx
-            gap_x = jnp.abs(cx - kx)
-            plane = empty
-            for j in range(groups):
-                inv = lax.rsqrt(square + flat[j])
-                lo = kx * per_x + 8 * j
-                coef = weight[lo : lo + 8] * (inv * inv * inv)
-                coef = jnp.where(jnp.maximum(gap_x, gaps[j]) >= 2, coef, 0.0)
-                sums[j] = sums[j] + coef
-                plane = plane + coef
-            fx = fx + rx * plane
-        fy, fall = empty, empty
-        for j in range(groups):
-            fy = fy + rys[j] * sums[j]
-            fall = fall + sums[j]
-        rows = empty
-        for k, value in enumerate((fx, fy, rz * fall)):
-            rows = jnp.where(sub == k, jnp.sum(value, 0, keepdims=True), rows)
-        own_acc[at_block(b), :] = acc[at_block(b), :] + FAR_COEF * rows
-        return 0
-
-    lax.fori_loop(0, blocks, far, 0, unroll=4)
+    own_acc[...] = acc[0 : 8 * blocks]
     for r in range(4):
         lo = 8 * (blocks + r * width)
         ghost_acc[r] = acc[lo : lo + 8 * width]
 
 
-def finish(width, slots, counts, own_acc, returned, out, acc):
+def finish(width, slots, counts, own_acc, returned, far, out, acc):
     blocks = own_acc.shape[0] // 8
-    acc[...] = own_acc[...]
+    acc[...] = own_acc[...] + far[...]
     for r in range(4):
 
         def add(g, _):
@@ -428,8 +437,6 @@
     slots = send_blocks.reshape(-1)
     counts = send_count.reshape(-1)
     cell = seg_cell.reshape(blocks, LANES)
-    here = lax.axis_index(ax) * ny + lax.axis_index(ay)
-    count = lax.dynamic_slice(pair_count, (here,), (1,))
     params = pltpu.CompilerParams(vmem_limit_bytes=VMEM_LIMIT)
 
     main, bz, terms, outgoing, local = pl.pallas_call(
@@ -471,9 +478,9 @@
     )(outgoing, local)
 
     own_acc, ghost_acc = pl.pallas_call(
-        functools.partial(interact, width),
+        functools.partial(interact, sizes, width),
         out_shape=(shape(blocks * 8, LANES), shape(4, 8 * width, LANES)),
-        in_specs=[SMEM_SPEC] * 2 + [VMEM_SPEC] * 6,
+        in_specs=[SMEM_SPEC] * 2 + [VMEM_SPEC] * 3,
         out_specs=(VMEM_SPEC,) * 2,
         scratch_shapes=[pltpu.VMEM(((blocks + 4 * width) * 8, LANES), F32)] * 3
         + [
@@ -483,29 +490,29 @@
         ],
         compiler_params=params,
         name="interact",
-    )(pair_list.reshape(-1), count, main, bz, ghosts, cell, terms, moments)
-
-    returned = pl.pallas_call(
+    )(pair_list.reshape(-1), pair_count, main, bz, ghosts)
+
+    returned, far = pl.pallas_call(
         functools.partial(give_back, sizes),
-        out_shape=shape(4, 8 * width, LANES),
-        in_specs=[VMEM_SPEC],
-        out_specs=VMEM_SPEC,
+        out_shape=(shape(4, 8 * width, LANES), shape(blocks * 8, LANES)),
+        in_specs=[VMEM_SPEC] * 5,
+        out_specs=(VMEM_SPEC,) * 2,
         scratch_shapes=[dma((4,)), dma((4,))],
         compiler_params=pltpu.CompilerParams(
             collective_id=1, has_side_effects=True, vmem_limit_bytes=VMEM_LIMIT
         ),
         name="give_back",
-    )(ghost_acc)
+    )(ghost_acc, main, cell, terms, moments)
 
     return pl.pallas_call(
         functools.partial(finish, width),
         out_shape=shape(6, seg_here),
-        in_specs=[SMEM_SPEC] * 2 + [VMEM_SPEC] * 2,
+        in_specs=[SMEM_SPEC] * 2 + [VMEM_SPEC] * 3,
         out_specs=VMEM_SPEC,
         scratch_shapes=[pltpu.VMEM((blocks * 8, LANES), F32)],
         compiler_params=params,
         name="finish",
-    )(slots, counts, own_acc, returned)
+    )(slots, counts, own_acc, returned, far)
 
 
 def solution(mesh):

time: 58.7 us -> 47.8 us (0.81); the launches traced: 58.6 us -> 46.8 us
  Pallas kernels: 53.3 us -> 41.9 us
    pallas_call x2, Pallas kernels: 35.8 us -> 24.5 us  [the longest x1 16.9 us: on_device(): pl.pallas_call(functools.partial(give_back, sizes), out_shape=(shape(4, 8...]
    reshape x1, local copies, waits for them, and re-layouts: 0.08 us -> 0.76 us  [on_device(): slots = send_blocks.reshape(-1)]
    unnamed x15 -> x13, local copies, waits for them, and re-layouts: 4.41 us -> 3.94 us
where the time goes in v4:
time: 47.8 us; the launch traced here: 46.8 us
  Pallas kernels  41.9 us (88%)
  local copies, waits for them, and re-layouts  4.83 us (10%)
    pallas_call x1, Pallas kernels, on_device(): pl.pallas_call(functools.partial(give_back, sizes), out_shape=(shape(4, 8...  16.9 us
    pallas_call x1, Pallas kernels, on_device(): pl.pallas_call(functools.partial(exchange, sizes), out_shape=(shape(4, se...  12.4 us
    pallas_call x1, Pallas kernels, on_device(): pl.pallas_call(functools.partial(interact, sizes, width), out_shape=(shap...  7.55 us
    unnamed x13, local copies, waits for them, and re-layouts  3.94 us
    pallas_call x1, Pallas kernels, on_device(): pl.pallas_call(functools.partial(prepare, width), out_shape=(shape(blocks...  3.36 us
    pallas_call x1, Pallas kernels, on_device(): pl.pallas_call(functools.partial(finish, width), out_shape=shape(6, seg_h...  1.76 us

profile of v4, /device:TPU:0, one launch (start us, length us, event | category | flops | bytes accessed | tf_op | source)
XLA Modules:
  0.0 46.8 jit_solution(519450021174345898)
XLA Ops:
  0.0 0.8 %reshape.12.slots = s32[96]{0:T(128)S(1)} reshape(s32[1,4,24]{2,1,0:T(4,128)} %param.10) | data formatting | bytes 768 | tf_op jit(solution)/shard_map/reshape | solution.py:437
  0.8 0.0 copy-start.5
  0.8 0.7 %copy-done.5 = s32[1,64,2]{1,2,0:T(2,128)S(1)} copy-done((s32[1,64,2]{1,2,0:T(2,128)S(1)}, s32[1,64,2]{1,2,0:T(2,128)}, u32[]{:S(2)}) %copy-start.5) | copy-done | bytes 536
  1.4 0.0 copy-start.2
  1.4 0.1 copy.9
  1.5 0.1 reshape.14.pairs
  1.7 0.0 copy-start.3
  1.7 0.5 %copy-done.2 = s32[8192]{0:T(1024)S(1)} copy-done((s32[8192]{0:T(1024)S(1)}, s32[8192]{0:T(1024)}, u32[]{:S(2)}) %copy-start.2) | copy-done | bytes 32792
  2.2 0.1 copy-done.3
  2.3 0.0 copy-start
  2.3 0.9 %copy-done = f32[6,8192]{1,0:T(8,128)S(1)} copy-done((f32[6,8192]{1,0:T(8,128)S(1)}, f32[6,8192]{1,0:T(8,128)}, u32[]{:S(2)}) %copy-start) | copy-done | bytes 196632
  3.3 0.0 copy-start.1
  3.3 0.9 %copy-done.1 = f32[3,8192]{1,0:T(4,128)S(1)} copy-done((f32[3,8192]{1,0:T(4,128)S(1)}, f32[3,8192]{1,0:T(4,128)}, u32[]{:S(2)}) %copy-start.1) | copy-done | bytes 98328
  4.2 3.4 %prepare.1 = (f32[512,128]{1,0:T(8,128)S(1)}, f32[64,128]{1,0:T(8,128)S(1)}, f32[16,8192]{1,0:T(8,128)S(1)}, f32[4,216,128]{2,1,0:T(8,128)S(1)}, f32[16,256]{1,0:T(8,128)S(1)}) custom-call(s32[96]{0:T(128)S(1)} %reshape.12.slots, s32[4]{0:T(128)S(1)} %bitcast.4, f32[6,8192]{1,0:T(8,128)S(1)} %copy-done, f32[3,8192]{1,0:T(4,128)S(1)} %copy-done.1, ...), custom_call_target="tpu_custom_call" | custom-call | tf_op jit(solution)/shard_map/prepare/pallas_call | solution.py:442
  7.6 12.4 %exchange.1 = (f32[4,216,128]{2,1,0:T(8,128)S(1)}, f32[16,256]{1,0:T(8,128)S(1)}) custom-call(f32[4,216,128]{2,1,0:T(8,128)S(1)} %get-tuple-element.18.outgoing, f32[16,256]{1,0:T(8,128)S(1)} %get-tuple-element.19.local), custom_call_target="tpu_custom_call" | custom-call | tf_op jit(solution)/shard_map/exchange/pallas_call | solution.py:458
  19.9 0.0 copy-start.4
  19.9 0.6 %copy-done.4 = s32[32]{0:T(128)S(1)} copy-done((s32[32]{0:T(128)S(1)}, s32[32]{0:T(128)}, u32[]{:S(2)}) %copy-start.4) | copy-done | bytes 152
  20.6 7.5 %interact.1 = (f32[512,128]{1,0:T(8,128)S(1)}, f32[4,192,128]{2,1,0:T(8,128)S(1)}) custom-call(s32[128]{0:T(128)S(1)} %reshape.14.pairs, s32[32]{0:T(128)S(1)} %copy-done.4, f32[512,128]{1,0:T(8,128)S(1)} %get-tuple-element.16.main, f32[64,128]{1,0:T(8,128)S(1)} %get-tuple-element.17.bz, f32[4,216,128]{2,1,0:T(8,128)S(1)} %get-tuple-element.20.ghosts), custom_call_target="tpu_custom_call" | custom-call | tf_op jit(solution)/shard_map/interact/pallas_call | solution.py:480
  28.1 16.9 %give_back.1 = (f32[4,192,128]{2,1,0:T(8,128)S(1)}, f32[512,128]{1,0:T(8,128)S(1)}) custom-call(f32[4,192,128]{2,1,0:T(8,128)S(1)} %get-tuple-element.22.forces, f32[512,128]{1,0:T(8,128)S(1)} %get-tuple-element.16.main, s32[64,128]{1,0:T(8,128)S(1)} %bitcast.3, f32[16,8192]{1,0:T(8,128)S(1)} %get-tuple-element.23.terms, f32[16,256]{1,0:T(8,128)S(1)} %get-tuple-element.24.moments), custom_call_target="tpu_custom_call" | custom-call | tf_op jit(solution)/shard_map/give_back/pallas_call | solution.py:495
  45.1 1.8 %finish.1 = f32[6,8192]{1,0:T(8,128)} custom-call(s32[96]{0:T(128)S(1)} %reshape.12.slots, s32[4]{0:T(128)S(1)} %bitcast.5, f32[512,128]{1,0:T(8,128)S(1)} %get-tuple-element.21.own_acc, f32[4,192,128]{2,1,0:T(8,128)S(1)} %get-tuple-element.25.returned, f32[512,128]{1,0:T(8,128)S(1)} %get-tuple-element.26.far), custom_call_target="tpu_custom_call" | custom-call | tf_op jit(solution)/shard_map/finish/pallas_call | solution.py:507
Async XLA Ops:
  0.8 0.7 %copy-start.5 = (s32[1,64,2]{1,2,0:T(2,128)S(1)}, s32[1,64,2]{1,2,0:T(2,128)}, u32[]{:S(2)}) copy-start(s32[1,64,2]{1,2,0:T(2,128)} %param.12) | copy-start | bytes 1540
  1.4 0.8 %copy-start.2 = (s32[8192]{0:T(1024)S(1)}, s32[8192]{0:T(1024)}, u32[]{:S(2)}) copy-start(s32[8192]{0:T(1024)} %param.9) | copy-start | bytes 98308
  1.7 0.7 %copy-start.3 = (s32[1,4]{1,0:T(1,128)S(1)}, s32[1,4]{1,0:T(1,128)}, u32[]{:S(2)}) copy-start(s32[1,4]{1,0:T(1,128)} %param.11) | copy-start | bytes 52
  2.3 0.9 %copy-start = (f32[6,8192]{1,0:T(8,128)S(1)}, f32[6,8192]{1,0:T(8,128)}, u32[]{:S(2)}) copy-start(f32[6,8192]{1,0:T(8,128)} %ends.1) | copy-start | bytes 589828
  3.3 0.9 %copy-start.1 = (f32[3,8192]{1,0:T(4,128)S(1)}, f32[3,8192]{1,0:T(4,128)}, u32[]{:S(2)}) copy-start(f32[3,8192]{1,0:T(4,128)} %burgers.1) | copy-start | bytes 294916
  19.9 0.7 %copy-start.4 = (s32[32]{0:T(128)S(1)}, s32[32]{0:T(128)}, u32[]{:S(2)}) copy-start(s32[32]{0:T(128)} %counts.1) | copy-start | bytes 388
